TPU v7x, 512 devices: a whole 4x4x16 slice. The times are simulated.
512 devices in a mesh: grp: 8 (over x, core), dev: 64 (over z, y).
Axes of the slice: x: 4, y: 4, z: 16, core: 2. Of those that a mesh axis runs over, the one named last changes fastest.
Arguments:
- embeddings: bfloat16 [196608, 1024], P(('grp', 'dev')), may hold values from -6 to 6
- cluster_ids: int32 [196608], P(('grp', 'dev')), may hold values from 0 to 255, never falling along the last dimension, each value on 1 to 1537 neighbouring positions
Outputs:
- neighbour_mean: float32 [196608, 1024], P(('grp', 'dev'))
- log_count: float32 [196608], P(('grp', 'dev'))
Inputs may be any that keep to these rules, and one draw needn't show every extreme that they name: cluster_ids never fall along the clips, so each cluster's clips are consecutive; each cluster has 1 to (5 - 1) * 384 + 1 clips and one has exactly that many; every cluster appears.
All inputs are finite; a program needn't handle non-finite values.
Results may differ from a plain program's by a relative error of at most 0.0078.
Values may be sent and summed in bfloat16 or wider, within the bound.
No kernel may reach another device: no remote copies, remote signals or barrier semaphores. Data moves between devices by JAX's collectives and lax.ppermute only.
A program may use at most 64 MiB of HBM per device.

v0:
```python
import math

import jax
import jax.numpy as jnp
from jax import lax
from jax.sharding import PartitionSpec as P

SPAN = 5


def passed_along(shard, axis, by):
    length = lax.axis_size(axis)
    pairs = [(i, i + by) for i in range(length) if 0 <= i + by < length]
    return lax.ppermute(shard, axis, pairs)


def pair_weights(left_rows, left_label, right_rows, right_label, kernel_scale, diagonal):
    scores = (
        lax.dot_general(
            left_rows, right_rows, (((1,), (1,)), ((), ())), preferred_element_type=jnp.float32
        )
        * kernel_scale
    )
    linked = left_label[:, None] == right_label[None, :]
    if diagonal:
        tile_size = left_rows.shape[0]
        linked = linked & (
            lax.broadcasted_iota(jnp.int32, (tile_size, tile_size), 0)
            != lax.broadcasted_iota(jnp.int32, (tile_size, tile_size), 1)
        )
    return jnp.where(linked, jnp.exp(scores), 0.0)


def tile_products(unit_rows, own_label, far_rows, far_label, kernel_scale):
    weight = pair_weights(unit_rows, own_label, far_rows, far_label, kernel_scale, False)
    rounded = weight.astype(jnp.bfloat16)
    row_pull = jnp.dot(rounded, far_rows, preferred_element_type=jnp.float32)
    row_count = jnp.sum(weight, axis=1)
    col_pull = lax.dot_general(
        rounded, unit_rows, (((0,), (0,)), ((), ())), preferred_element_type=jnp.float32
    )
    return (row_pull, row_count, col_pull, jnp.sum(weight, axis=0))


def shards(embeddings, cluster_ids):
    tile_rows, feat_width = embeddings.shape
    kernel_scale = 2.0 / math.sqrt(feat_width)
    values = embeddings.astype(jnp.float32)
    unit_rows = (
        values * lax.rsqrt(jnp.mean(values * values, axis=1, keepdims=True) + 1e-06)
    ).astype(jnp.bfloat16)
    own_label = (cluster_ids + 1).astype(jnp.bfloat16)
    own_weight = pair_weights(unit_rows, own_label, unit_rows, own_label, kernel_scale, True)
    pulled = jnp.dot(own_weight.astype(jnp.bfloat16), unit_rows, preferred_element_type=jnp.float32)
    counted = jnp.sum(own_weight, axis=1)
    far_rows, far_label = (unit_rows, own_label)
    for distance in range(1, SPAN):
        far_rows, far_label = passed_along((unit_rows, own_label), ("grp", "dev"), -distance)
        row_pull, row_count, col_pull, col_count = tile_products(
            unit_rows, own_label, far_rows, far_label, kernel_scale
        )
        pulled = pulled + row_pull
        counted = counted + row_count
        back_pull, back_count = passed_along((col_pull, col_count), ("grp", "dev"), distance)
        pulled = pulled + back_pull
        counted = counted + back_count
    neighbour_mean = pulled / (1.0 + counted)[:, None]
    return (neighbour_mean, jnp.log(1.0 + counted))


def solution(mesh):
    placed = (P(("grp", "dev"), None), P(("grp", "dev")))
    return jax.shard_map(
        shards,
        mesh=mesh,
        in_specs=placed,
        out_specs=(P(("grp", "dev"), None), P(("grp", "dev"))),
        check_vma=False,
    )
```

profile of v0, /device:TPU:6, one launch (start us, length us, event | category | flops | bytes accessed | tf_op | source)
XLA Modules:
  0.0 308.4 jit_solution(2211859251368356397)
XLA Ops:
  0.6 0.0 copy-start
  0.6 1.4 fusion
  2.0 1.3 fusion.1
  3.4 12.1 %collective-permute-start.7 = (bf16[384,1024]{1,0:T(8,128)(2,1)S(1)}, bf16[384,1024]{1,0:T(8,128)(2,1)S(1)}, u32[]{:S(2)}, u32[]{:S(2)}) collective-permute-start(bf16[384,1024]{1,0:T(8,128)(2,1)S(1)} %fusion.1), channel_id=1, source_target_pairs={{3,0},{4,1},{5,2},{6,3},{7,4},{8,5},{9,6},{10,7},{11,8},{12,9},{13... | collective-permute-start | bytes 2359304 | tf_op jit(solution)/shard_map/ppermute | solution.py:14
  15.5 5.0 %collective-permute-start.4 = (bf16[384,1024]{1,0:T(8,128)(2,1)S(1)}, bf16[384,1024]{1,0:T(8,128)(2,1)S(1)}, u32[]{:S(2)}, u32[]{:S(2)}) collective-permute-start(bf16[384,1024]{1,0:T(8,128)(2,1)S(1)} %fusion.1), channel_id=1, source_target_pairs={{2,0},{3,1},{4,2},{5,3},{6,4},{7,5},{8,6},{9,7},{10,8},{11,9},{12,... | collective-permute-start | bytes 2359304 | tf_op jit(solution)/shard_map/ppermute | solution.py:14
  20.5 2.6 collective-permute-start.10
  23.1 0.0 copy-done
  23.1 3.0 collective-permute-start
  26.1 2.0 collective-permute-start.3
  28.2 0.7 fusion.40
  28.8 4.6 %collective-permute-done.7 = bf16[384,1024]{1,0:T(8,128)(2,1)S(1)} collective-permute-done((bf16[384,1024]{1,0:T(8,128)(2,1)S(1)}, bf16[384,1024]{1,0:T(8,128)(2,1)S(1)}, u32[]{:S(2)}, u32[]{:S(2)}) %collective-permute-start.7) | collective-permute-done | bytes 786464 | tf_op jit(solution)/shard_map/ppermute | solution.py:14
  33.4 8.5 %collective-permute-start.1 = (bf16[384,1024]{1,0:T(8,128)(2,1)S(1)}, bf16[384,1024]{1,0:T(8,128)(2,1)S(1)}, u32[]{:S(2)}, u32[]{:S(2)}) collective-permute-start(bf16[384,1024]{1,0:T(8,128)(2,1)S(1)} %fusion.1), channel_id=1, source_target_pairs={{1,0},{2,1},{3,2},{4,3},{5,4},{6,5},{7,6},{8,7},{9,8},{10,9},{11,1... | collective-permute-start | bytes 2359304 | tf_op jit(solution)/shard_map/ppermute | solution.py:14
  41.9 0.6 fusion.3
  42.6 7.7 %collective-permute-done.4 = bf16[384,1024]{1,0:T(8,128)(2,1)S(1)} collective-permute-done((bf16[384,1024]{1,0:T(8,128)(2,1)S(1)}, bf16[384,1024]{1,0:T(8,128)(2,1)S(1)}, u32[]{:S(2)}, u32[]{:S(2)}) %collective-permute-start.4) | collective-permute-done | bytes 786464 | tf_op jit(solution)/shard_map/ppermute | solution.py:14
  50.2 2.0 collective-permute-start.6
  52.2 0.6 fusion.4
  52.8 14.3 %collective-permute-done.10 = bf16[384,1024]{1,0:T(8,128)(2,1)S(1)} collective-permute-done((bf16[384,1024]{1,0:T(8,128)(2,1)S(1)}, bf16[384,1024]{1,0:T(8,128)(2,1)S(1)}, u32[]{:S(2)}, u32[]{:S(2)}) %collective-permute-start.10) | collective-permute-done | bytes 786464 | tf_op jit(solution)/shard_map/ppermute | solution.py:14
  67.1 5.9 %collective-permute-start.9 = (bf16[384]{0:T(512)(128)(2,1)S(1)}, bf16[384]{0:T(512)(128)(2,1)S(1)}, u32[]{:S(2)}, u32[]{:S(2)}) collective-permute-start(bf16[384]{0:T(512)(128)(2,1)S(1)} %add_convert_fusion), channel_id=1, source_target_pairs={{4,0},{5,1},{6,2},{7,3},{8,4},{9,5},{10,6},{11,7},{12,8},{13,9},{1... | collective-permute-start | bytes 2312 | tf_op jit(solution)/shard_map/ppermute | solution.py:14
  73.0 0.6 fusion.2
  73.6 0.0 collective-permute-done
  73.6 0.0 collective-permute-done.3
  73.7 10.1 %collective-permute-done.6 = bf16[384]{0:T(512)(128)(2,1)S(1)} collective-permute-done((bf16[384]{0:T(512)(128)(2,1)S(1)}, bf16[384]{0:T(512)(128)(2,1)S(1)}, u32[]{:S(2)}, u32[]{:S(2)}) %collective-permute-start.6) | collective-permute-done | bytes 800 | tf_op jit(solution)/shard_map/ppermute | solution.py:14
  83.8 0.0 collective-permute-done.9
  83.8 0.0 collective-permute-done.1
  83.8 0.9 fusion.10
  84.6 0.6 fusion.35
  85.3 1.9 collective-permute-start.2
  87.2 0.6 fusion.31
  87.8 1.9 collective-permute-start.5
  89.7 0.6 fusion.27
  90.4 1.9 collective-permute-start.8
  92.3 0.6 fusion.23
  92.9 1.9 collective-permute-start.11
  94.8 0.6 fusion.21
  95.5 3.6 %collective-permute-start.12 = (f32[384]{0:T(512)S(1)}, f32[384]{0:T(512)S(1)}, u32[]{:S(2)}, u32[]{:S(2)}) collective-permute-start(f32[384]{0:T(512)S(1)} %get-tuple-element.3), channel_id=1, source_target_pairs={{0,1},{1,2},{2,3},{3,4},{4,5},{5,6},{6,7},{7,8},{8,9},{9,10},{10,1... | collective-permute-start | bytes 4616 | tf_op jit(solution)/shard_map/ppermute | solution.py:14
  99.1 0.7 fusion.29
  99.8 174.3 %collective-permute-done.12 = f32[384]{0:T(512)S(1)} collective-permute-done((f32[384]{0:T(512)S(1)}, f32[384]{0:T(512)S(1)}, u32[]{:S(2)}, u32[]{:S(2)}) %collective-permute-start.12) | collective-permute-done | bytes 1568 | tf_op jit(solution)/shard_map/ppermute | solution.py:14
  274.1 1.9 collective-permute-start.13
  276.0 0.7 fusion.33
  276.7 6.8 %collective-permute-done.13 = f32[384]{0:T(512)S(1)} collective-permute-done((f32[384]{0:T(512)S(1)}, f32[384]{0:T(512)S(1)}, u32[]{:S(2)}, u32[]{:S(2)}) %collective-permute-start.13) | collective-permute-done | bytes 1568 | tf_op jit(solution)/shard_map/ppermute | solution.py:14
  283.5 1.9 collective-permute-start.14
  285.4 0.7 fusion.25
  286.1 9.6 %collective-permute-done.14 = f32[384]{0:T(512)S(1)} collective-permute-done((f32[384]{0:T(512)S(1)}, f32[384]{0:T(512)S(1)}, u32[]{:S(2)}, u32[]{:S(2)}) %collective-permute-start.14) | collective-permute-done | bytes 1568 | tf_op jit(solution)/shard_map/ppermute | solution.py:14
  295.7 1.9 collective-permute-start.15
  297.6 0.7 fusion.37
  298.3 6.6 %collective-permute-done.15 = f32[384]{0:T(512)S(1)} collective-permute-done((f32[384]{0:T(512)S(1)}, f32[384]{0:T(512)S(1)}, u32[]{:S(2)}, u32[]{:S(2)}) %collective-permute-start.15) | collective-permute-done | bytes 1568 | tf_op jit(solution)/shard_map/ppermute | solution.py:14
  304.9 0.6 fusion.39
  305.5 0.0 collective-permute-done.2
  305.5 0.0 collective-permute-done.5
  305.5 0.0 collective-permute-done.8
  305.5 0.0 collective-permute-done.11
  305.5 2.9 add_divide_fusion
  (2 shorter events, 0.0 us)
Async XLA Ops:
  0.6 22.5 %copy-start = (s32[384]{0:T(512)S(1)}, s32[384]{0:T(512)}, u32[]{:S(2)}) copy-start(s32[384]{0:T(512)} %param.3) | copy-start | bytes 4612
  3.4 30.0 %collective-permute-start.7 = (bf16[384,1024]{1,0:T(8,128)(2,1)S(1)}, bf16[384,1024]{1,0:T(8,128)(2,1)S(1)}, u32[]{:S(2)}, u32[]{:S(2)}) collective-permute-start(bf16[384,1024]{1,0:T(8,128)(2,1)S(1)} %fusion.1), channel_id=1, source_target_pairs={{3,0},{4,1},{5,2},{6,3},{7,4},{8,5},{9,6},{10,7},{11,8},{12,9},{13... | collective-permute-start | bytes 2359304 | tf_op jit(solution)/shard_map/ppermute | solution.py:14
  15.5 34.8 %collective-permute-start.4 = (bf16[384,1024]{1,0:T(8,128)(2,1)S(1)}, bf16[384,1024]{1,0:T(8,128)(2,1)S(1)}, u32[]{:S(2)}, u32[]{:S(2)}) collective-permute-start(bf16[384,1024]{1,0:T(8,128)(2,1)S(1)} %fusion.1), channel_id=1, source_target_pairs={{2,0},{3,1},{4,2},{5,3},{6,4},{7,5},{8,6},{9,7},{10,8},{11,9},{12,... | collective-permute-start | bytes 2359304 | tf_op jit(solution)/shard_map/ppermute | solution.py:14
  20.5 46.6 %collective-permute-start.10 = (bf16[384,1024]{1,0:T(8,128)(2,1)S(1)}, bf16[384,1024]{1,0:T(8,128)(2,1)S(1)}, u32[]{:S(2)}, u32[]{:S(2)}) collective-permute-start(bf16[384,1024]{1,0:T(8,128)(2,1)S(1)} %fusion.1), channel_id=1, source_target_pairs={{4,0},{5,1},{6,2},{7,3},{8,4},{9,5},{10,6},{11,7},{12,8},{13,9},{1... | collective-permute-start | bytes 2359304 | tf_op jit(solution)/shard_map/ppermute | solution.py:14
  23.1 50.5 %collective-permute-start = (bf16[384]{0:T(512)(128)(2,1)S(1)}, bf16[384]{0:T(512)(128)(2,1)S(1)}, u32[]{:S(2)}, u32[]{:S(2)}) collective-permute-start(bf16[384]{0:T(512)(128)(2,1)S(1)} %add_convert_fusion), channel_id=1, source_target_pairs={{1,0},{2,1},{3,2},{4,3},{5,4},{6,5},{7,6},{8,7},{9,8},{10,9},{11,1... | collective-permute-start | bytes 2312 | tf_op jit(solution)/shard_map/ppermute | solution.py:14
  26.1 47.5 %collective-permute-start.3 = (bf16[384]{0:T(512)(128)(2,1)S(1)}, bf16[384]{0:T(512)(128)(2,1)S(1)}, u32[]{:S(2)}, u32[]{:S(2)}) collective-permute-start(bf16[384]{0:T(512)(128)(2,1)S(1)} %add_convert_fusion), channel_id=1, source_target_pairs={{2,0},{3,1},{4,2},{5,3},{6,4},{7,5},{8,6},{9,7},{10,8},{11,9},{12,... | collective-permute-start | bytes 2312 | tf_op jit(solution)/shard_map/ppermute | solution.py:14
  33.4 50.4 %collective-permute-start.1 = (bf16[384,1024]{1,0:T(8,128)(2,1)S(1)}, bf16[384,1024]{1,0:T(8,128)(2,1)S(1)}, u32[]{:S(2)}, u32[]{:S(2)}) collective-permute-start(bf16[384,1024]{1,0:T(8,128)(2,1)S(1)} %fusion.1), channel_id=1, source_target_pairs={{1,0},{2,1},{3,2},{4,3},{5,4},{6,5},{7,6},{8,7},{9,8},{10,9},{11,1... | collective-permute-start | bytes 2359304 | tf_op jit(solution)/shard_map/ppermute | solution.py:14
  50.2 33.5 %collective-permute-start.6 = (bf16[384]{0:T(512)(128)(2,1)S(1)}, bf16[384]{0:T(512)(128)(2,1)S(1)}, u32[]{:S(2)}, u32[]{:S(2)}) collective-permute-start(bf16[384]{0:T(512)(128)(2,1)S(1)} %add_convert_fusion), channel_id=1, source_target_pairs={{3,0},{4,1},{5,2},{6,3},{7,4},{8,5},{9,6},{10,7},{11,8},{12,9},{13... | collective-permute-start | bytes 2312 | tf_op jit(solution)/shard_map/ppermute | solution.py:14
  67.1 16.7 %collective-permute-start.9 = (bf16[384]{0:T(512)(128)(2,1)S(1)}, bf16[384]{0:T(512)(128)(2,1)S(1)}, u32[]{:S(2)}, u32[]{:S(2)}) collective-permute-start(bf16[384]{0:T(512)(128)(2,1)S(1)} %add_convert_fusion), channel_id=1, source_target_pairs={{4,0},{5,1},{6,2},{7,3},{8,4},{9,5},{10,6},{11,7},{12,8},{13,9},{1... | collective-permute-start | bytes 2312 | tf_op jit(solution)/shard_map/ppermute | solution.py:14
  85.3 220.2 %collective-permute-start.2 = (f32[384,1024]{1,0:T(8,128)S(1)}, f32[384,1024]{1,0:T(8,128)S(1)}, u32[]{:S(2)}, u32[]{:S(2)}) collective-permute-start(f32[384,1024]{1,0:T(8,128)S(1)} %fusion.35), channel_id=1, source_target_pairs={{0,1},{1,2},{2,3},{3,4},{4,5},{5,6},{6,7},{7,8},{8,9},{9,10},{10,1... | collective-permute-start | bytes 4718600 | tf_op jit(solution)/shard_map/ppermute | solution.py:14
  87.8 217.7 %collective-permute-start.5 = (f32[384,1024]{1,0:T(8,128)S(1)}, f32[384,1024]{1,0:T(8,128)S(1)}, u32[]{:S(2)}, u32[]{:S(2)}) collective-permute-start(f32[384,1024]{1,0:T(8,128)S(1)} %fusion.31), channel_id=1, source_target_pairs={{0,2},{1,3},{2,4},{3,5},{4,6},{5,7},{6,8},{7,9},{8,10},{9,11},{10,... | collective-permute-start | bytes 4718600 | tf_op jit(solution)/shard_map/ppermute | solution.py:14
  90.4 215.1 %collective-permute-start.8 = (f32[384,1024]{1,0:T(8,128)S(1)}, f32[384,1024]{1,0:T(8,128)S(1)}, u32[]{:S(2)}, u32[]{:S(2)}) collective-permute-start(f32[384,1024]{1,0:T(8,128)S(1)} %fusion.27), channel_id=1, source_target_pairs={{0,3},{1,4},{2,5},{3,6},{4,7},{5,8},{6,9},{7,10},{8,11},{9,12},{10... | collective-permute-start | bytes 4718600 | tf_op jit(solution)/shard_map/ppermute | solution.py:14
  92.9 212.6 %collective-permute-start.11 = (f32[384,1024]{1,0:T(8,128)S(1)}, f32[384,1024]{1,0:T(8,128)S(1)}, u32[]{:S(2)}, u32[]{:S(2)}) collective-permute-start(f32[384,1024]{1,0:T(8,128)S(1)} %fusion.23), channel_id=1, source_target_pairs={{0,4},{1,5},{2,6},{3,7},{4,8},{5,9},{6,10},{7,11},{8,12},{9,13},{1... | collective-permute-start | bytes 4718600 | tf_op jit(solution)/shard_map/ppermute | solution.py:14
  95.5 178.6 %collective-permute-start.12 = (f32[384]{0:T(512)S(1)}, f32[384]{0:T(512)S(1)}, u32[]{:S(2)}, u32[]{:S(2)}) collective-permute-start(f32[384]{0:T(512)S(1)} %get-tuple-element.3), channel_id=1, source_target_pairs={{0,1},{1,2},{2,3},{3,4},{4,5},{5,6},{6,7},{7,8},{8,9},{9,10},{10,1... | collective-permute-start | bytes 4616 | tf_op jit(solution)/shard_map/ppermute | solution.py:14
  274.1 9.4 %collective-permute-start.13 = (f32[384]{0:T(512)S(1)}, f32[384]{0:T(512)S(1)}, u32[]{:S(2)}, u32[]{:S(2)}) collective-permute-start(f32[384]{0:T(512)S(1)} %get-tuple-element.10), channel_id=1, source_target_pairs={{0,2},{1,3},{2,4},{3,5},{4,6},{5,7},{6,8},{7,9},{8,10},{9,11},{10,... | collective-permute-start | bytes 4616 | tf_op jit(solution)/shard_map/ppermute | solution.py:14
  283.5 12.2 %collective-permute-start.14 = (f32[384]{0:T(512)S(1)}, f32[384]{0:T(512)S(1)}, u32[]{:S(2)}, u32[]{:S(2)}) collective-permute-start(f32[384]{0:T(512)S(1)} %get-tuple-element.12), channel_id=1, source_target_pairs={{0,3},{1,4},{2,5},{3,6},{4,7},{5,8},{6,9},{7,10},{8,11},{9,12},{10... | collective-permute-start | bytes 4616 | tf_op jit(solution)/shard_map/ppermute | solution.py:14
  295.7 9.2 %collective-permute-start.15 = (f32[384]{0:T(512)S(1)}, f32[384]{0:T(512)S(1)}, u32[]{:S(2)}, u32[]{:S(2)}) collective-permute-start(f32[384]{0:T(512)S(1)} %get-tuple-element.14), channel_id=1, source_target_pairs={{0,4},{1,5},{2,6},{3,7},{4,8},{5,9},{6,10},{7,11},{8,12},{9,13},{1... | collective-permute-start | bytes 4616 | tf_op jit(solution)/shard_map/ppermute | solution.py:14
where the time goes:
time: 313 us; the launch traced here: 308 us
  waiting for transfers between devices  234 us (75%)
  starting transfers between devices  58.2 us (19%)
  matrix products  9.15 us (3%)
  other arithmetic  6.21 us (2%)
    ppermute x16, waiting for transfers between devices, passed_along(): return lax.ppermute(shard, axis, pairs)  234 us
    ppermute x16, starting transfers between devices, passed_along(): return lax.ppermute(shard, axis, pairs)  58.2 us
  transfers between devices with their start and end apart: 16, of which 8 were waited for; matrix products, arithmetic and copies ran while one was open for 3% of the time, Pallas kernels for 0%

commit v1 on v0

v1 whole, which is shorter than its diff:
```python
import math

import jax
import jax.numpy as jnp
from jax import lax
from jax.experimental import pallas as pl
from jax.experimental.pallas import tpu as pltpu
from jax.sharding import PartitionSpec as P

AXES = ("grp", "dev")
RING = 4
TAIL = 16
VMEM_BYTES = 40 * 1024 * 1024


def plane_pairs(total, up, along, columns=range(RING)):
    pairs = []
    for plane in range(total // RING):
        if 0 <= plane + up < total // RING:
            for column in columns:
                target = (column + along) % RING
                pairs.append((plane * RING + column, (plane + up) * RING + target))
    return pairs


def send(block, pairs):
    return lax.ppermute(block, AXES, pairs)


def pack_kernel(values_ref, label_ref, packed_ref):
    rows, width = values_ref.shape
    values = values_ref[...].astype(jnp.float32)
    scale = lax.rsqrt(jnp.mean(values * values, axis=1, keepdims=True) + 1e-06)
    packed_ref[:rows, :] = (values * scale).astype(jnp.bfloat16)
    label = (label_ref[...] + 1).astype(jnp.float32).astype(jnp.bfloat16)
    packed_ref[rows:, :rows] = jnp.broadcast_to(label, (TAIL, rows))
    packed_ref[rows:, rows:] = jnp.zeros((TAIL, width - rows), jnp.bfloat16)


def tile(own, own_label, far_ref, kernel_scale, diagonal):
    rows = own.shape[0]
    far = far_ref[:rows, :]
    far_label = far_ref[rows : rows + TAIL, :rows].astype(jnp.float32)[:1, :]
    scores = (
        lax.dot_general(own, far, (((1,), (1,)), ((), ())), preferred_element_type=jnp.float32)
        * kernel_scale
    )
    linked = own_label == far_label
    if diagonal:
        linked = linked & (
            lax.broadcasted_iota(jnp.int32, (rows, rows), 0)
            != lax.broadcasted_iota(jnp.int32, (rows, rows), 1)
        )
    weight = jnp.where(linked, jnp.exp(scores), 0.0)
    pull = jnp.dot(weight.astype(jnp.bfloat16), far, preferred_element_type=jnp.float32)
    return pull, jnp.sum(weight, axis=1, keepdims=True)


def first_kernel(kernel_scale, own_ref, *refs):
    far_refs, (pulled_ref, counted_ref) = refs[:-2], refs[-2:]
    rows = pulled_ref.shape[0]
    own = own_ref[:rows, :]
    label = own_ref[rows:, :rows].astype(jnp.float32)[:1, :]
    own_label = jnp.broadcast_to(label, (128, rows)).T[:, :1]
    pulled, counted = tile(own, own_label, own_ref, kernel_scale, True)
    for far_ref in far_refs:
        pull, count = tile(own, own_label, far_ref, kernel_scale, False)
        pulled, counted = pulled + pull, counted + count
    pulled_ref[...] = pulled
    counted_ref[...] = jnp.broadcast_to(counted, counted_ref.shape)


def last_kernel(kernel_scale, own_ref, pulled_ref, counted_ref, *refs):
    far_refs, (mean_ref, log_ref) = refs[:-2], refs[-2:]
    rows = pulled_ref.shape[0]
    own = own_ref[:rows, :]
    label = own_ref[rows:, :rows].astype(jnp.float32)[:1, :]
    own_label = jnp.broadcast_to(label, (128, rows)).T[:, :1]
    pulled, counted = pulled_ref[...], counted_ref[:, :1]
    for far_ref in far_refs:
        pull, count = tile(own, own_label, far_ref, kernel_scale, False)
        pulled, counted = pulled + pull, counted + count
    mean_ref[...] = pulled / (1.0 + counted)
    log_ref[...] = jnp.log(1.0 + jnp.broadcast_to(counted, (rows, 128)).T[:1, :])


def cost(tiles, rows, width):
    return pl.CostEstimate(
        flops=4 * tiles * rows * rows * width,
        bytes_accessed=2 * (tiles + 1) * rows * width,
        transcendentals=tiles * rows * rows,
    )


def shards(embeddings, cluster_ids):
    rows, width = embeddings.shape
    total = lax.axis_size("grp") * lax.axis_size("dev")
    kernel_scale = 2.0 / math.sqrt(width)
    params = pltpu.CompilerParams(vmem_limit_bytes=VMEM_BYTES)
    own = pl.pallas_call(
        pack_kernel,
        out_shape=jax.ShapeDtypeStruct((rows + TAIL, width), jnp.bfloat16),
        compiler_params=params,
        name="pack",
    )(embeddings, cluster_ids.reshape(1, rows))
    column = lax.rem(lax.axis_index("dev"), RING)

    below = send(own, plane_pairs(total, 1, 0))
    above = send(own, plane_pairs(total, -1, 0))
    across = send(own, plane_pairs(total, 0, 2))
    left = send(own, plane_pairs(total, 0, 1))
    right = send(own, plane_pairs(total, 0, -1))
    side_down = send(jnp.where(column == 0, above, below), plane_pairs(total, 0, -1))
    side_up = send(jnp.where(column == RING - 1, below, above), plane_pairs(total, 0, 1))
    corner = send(
        across,
        plane_pairs(total, 1, 0, range(RING // 2))
        + plane_pairs(total, -1, 0, range(RING // 2, RING)),
    )

    near = (below, above, left, right, across)
    pulled, counted = pl.pallas_call(
        lambda *refs: first_kernel(kernel_scale, *refs),
        out_shape=(
            jax.ShapeDtypeStruct((rows, width), jnp.float32),
            jax.ShapeDtypeStruct((rows, 128), jnp.float32),
        ),
        compiler_params=params,
        cost_estimate=cost(1 + len(near), rows, width),
        name="near",
    )(own, *near)
    late = (side_down, side_up, corner)
    neighbour_mean, log_count = pl.pallas_call(
        lambda *refs: last_kernel(kernel_scale, *refs),
        out_shape=(
            jax.ShapeDtypeStruct((rows, width), jnp.float32),
            jax.ShapeDtypeStruct((1, rows), jnp.float32),
        ),
        compiler_params=params,
        cost_estimate=cost(len(late), rows, width),
        name="late",
    )(own, pulled, counted, *late)
    return neighbour_mean, log_count.reshape(rows)


def solution(mesh):
    placed = (P(AXES, None), P(AXES))
    return jax.shard_map(
        shards,
        mesh=mesh,
        in_specs=placed,
        out_specs=placed,
        check_vma=False,
    )
```

time: 313 us -> 80.2 us (0.26); the launches traced: 308 us -> 79.8 us
  waiting for transfers between devices: 234 us -> 31.5 us
  starting transfers between devices: 58.2 us -> 33.9 us
  Pallas kernels: 0 us -> 11.1 us
  matrix products: 9.15 us -> 0 us
  other arithmetic: 6.21 us -> 0.71 us
    ppermute x16 -> x8, waiting for transfers between devices: 234 us -> 31.5 us  [send(): return lax.ppermute(block, AXES, pairs)]
    ppermute x16 -> x8, starting transfers between devices: 58.2 us -> 33.9 us  [send(): return lax.ppermute(block, AXES, pairs)]
    pallas_call x0 -> x3, Pallas kernels: none -> 11.1 us  [the longest x1 6.82 us: shards(): pl.pallas_call(lambda *refs: first_kernel(kernel_scale, *refs), out_shape...]
    dot_general x14 -> x0, matrix products: 9.15 us -> none  [the longest x5 3.35 us: pair_weights(): lax.dot_general(left_rows, right_rows, (((1,), (1,)), ((), ())), preferre...]
  transfers between devices with their start and end apart: 16 -> 8, of which waited for: 8 -> 5; matrix products, arithmetic and copies ran while one was open for 3% -> 0% of each run, Pallas kernels for 0% -> 9%
where the time goes in v1:
time: 80.2 us; the launch traced here: 79.8 us
  starting transfers between devices  33.9 us (42%)
  waiting for transfers between devices  31.5 us (39%)
  Pallas kernels  11.1 us (14%)
  local copies, waits for them, and re-layouts  1.82 us (2%)
    ppermute x8, starting transfers between devices, send(): return lax.ppermute(block, AXES, pairs)  33.9 us
    ppermute x8, waiting for transfers between devices, send(): return lax.ppermute(block, AXES, pairs)  31.5 us
    pallas_call x1, Pallas kernels, shards(): pl.pallas_call(lambda *refs: first_kernel(kernel_scale, *refs), out_shape...  6.82 us
    pallas_call x1, Pallas kernels, shards(): pl.pallas_call(lambda *refs: last_kernel(kernel_scale, *refs), out_shape=...  4 us
  transfers between devices with their start and end apart: 8, of which 5 were waited for; matrix products, arithmetic and copies ran while one was open for 0% of the time, Pallas kernels for 9%

profile of v1, /device:TPU:6, one launch (start us, length us, event | category | flops | bytes accessed | tf_op | source)
XLA Modules:
  0.0 79.8 jit_solution(3730460846465200197)
XLA Ops:
  0.6 0.7 reshape.10.label_ref
  1.3 0.0 copy-start
  1.3 1.1 %copy-done = bf16[384,1024]{1,0:T(8,128)(2,1)S(1)} copy-done((bf16[384,1024]{1,0:T(8,128)(2,1)S(1)}, bf16[384,1024]{1,0:T(8,128)(2,1)}, u32[]{:S(2)}) %copy-start) | copy-done | bytes 786456
  2.4 0.2 pack.1.refs_0_
  2.7 3.8 %collective-permute-start = (bf16[400,1024]{1,0:T(8,128)(2,1)S(1)}, bf16[400,1024]{1,0:T(8,128)(2,1)S(1)}, u32[]{:S(2)}, u32[]{:S(2)}) collective-permute-start(bf16[400,1024]{1,0:T(8,128)(2,1)S(1)} %pack.1.refs_0_), channel_id=1, source_target_pairs={{0,4},{1,5},{2,6},{3,7},{4,8},{5,9},{6,10},{7,11},{8,12},{9,13},{1... | collective-permute-start | bytes 2457608 | tf_op jit(solution)/shard_map/ppermute | solution.py:27
  6.5 9.2 %collective-permute-start.1 = (bf16[400,1024]{1,0:T(8,128)(2,1)S(1)}, bf16[400,1024]{1,0:T(8,128)(2,1)S(1)}, u32[]{:S(2)}, u32[]{:S(2)}) collective-permute-start(bf16[400,1024]{1,0:T(8,128)(2,1)S(1)} %pack.1.refs_0_), channel_id=1, source_target_pairs={{4,0},{5,1},{6,2},{7,3},{8,4},{9,5},{10,6},{11,7},{12,8},{13,9},{1... | collective-permute-start | bytes 2457608 | tf_op jit(solution)/shard_map/ppermute | solution.py:27
  15.7 5.1 %collective-permute-start.4 = (bf16[400,1024]{1,0:T(8,128)(2,1)S(1)}, bf16[400,1024]{1,0:T(8,128)(2,1)S(1)}, u32[]{:S(2)}, u32[]{:S(2)}) collective-permute-start(bf16[400,1024]{1,0:T(8,128)(2,1)S(1)} %pack.1.refs_0_), channel_id=1, source_target_pairs={{0,2},{1,3},{2,0},{3,1},{4,6},{5,7},{6,4},{7,5},{8,10},{9,11},{10,... | collective-permute-start | bytes 2457608 | tf_op jit(solution)/shard_map/ppermute | solution.py:27
  20.9 2.6 %collective-permute-start.2 = (bf16[400,1024]{1,0:T(8,128)(2,1)S(1)}, bf16[400,1024]{1,0:T(8,128)(2,1)}, u32[]{:S(2)}, u32[]{:S(2)}) collective-permute-start(bf16[400,1024]{1,0:T(8,128)(2,1)S(1)} %pack.1.refs_0_), channel_id=1, source_target_pairs={{0,1},{1,2},{2,3},{3,0},{4,5},{5,6},{6,7},{7,4},{8,9},{9,10},{10,1... | collective-permute-start | bytes 2457608 | tf_op jit(solution)/shard_map/ppermute | solution.py:27
  23.4 4.5 %collective-permute-start.3 = (bf16[400,1024]{1,0:T(8,128)(2,1)S(1)}, bf16[400,1024]{1,0:T(8,128)(2,1)}, u32[]{:S(2)}, u32[]{:S(2)}) collective-permute-start(bf16[400,1024]{1,0:T(8,128)(2,1)S(1)} %pack.1.refs_0_), channel_id=1, source_target_pairs={{0,3},{1,0},{2,1},{3,2},{4,7},{5,4},{6,5},{7,6},{8,11},{9,8},{10,9... | collective-permute-start | bytes 2457608 | tf_op jit(solution)/shard_map/ppermute | solution.py:27
  27.9 3.8 %collective-permute-done.refs_1_ = bf16[400,1024]{1,0:T(8,128)(2,1)S(1)} collective-permute-done((bf16[400,1024]{1,0:T(8,128)(2,1)S(1)}, bf16[400,1024]{1,0:T(8,128)(2,1)S(1)}, u32[]{:S(2)}, u32[]{:S(2)}) %collective-permute-start) | collective-permute-done | bytes 819232 | tf_op jit(solution)/shard_map/ppermute | solution.py:27
  31.8 2.3 %collective-permute-done.1.refs_2_ = bf16[400,1024]{1,0:T(8,128)(2,1)S(1)} collective-permute-done((bf16[400,1024]{1,0:T(8,128)(2,1)S(1)}, bf16[400,1024]{1,0:T(8,128)(2,1)S(1)}, u32[]{:S(2)}, u32[]{:S(2)}) %collective-permute-start.1) | collective-permute-done | bytes 819232 | tf_op jit(solution)/shard_map/ppermute | solution.py:27
  34.1 0.1 broadcast_select_fusion
  34.2 4.9 %collective-permute-start.5 = (bf16[400,1024]{1,0:T(8,128)(2,1)S(1)}, bf16[400,1024]{1,0:T(8,128)(2,1)S(1)}, u32[]{:S(2)}, u32[]{:S(2)}) collective-permute-start(bf16[400,1024]{1,0:T(8,128)(2,1)S(1)} %get-tuple-element.11), channel_id=1, source_target_pairs={{0,3},{1,0},{2,1},{3,2},{4,7},{5,4},{6,5},{7,6},{8,11},{9,8},{10,9... | collective-permute-start | bytes 2457608 | tf_op jit(solution)/shard_map/ppermute | solution.py:27
  39.1 1.9 %collective-permute-start.6 = (bf16[400,1024]{1,0:T(8,128)(2,1)S(1)}, bf16[400,1024]{1,0:T(8,128)(2,1)S(1)}, u32[]{:S(2)}, u32[]{:S(2)}) collective-permute-start(bf16[400,1024]{1,0:T(8,128)(2,1)S(1)} %get-tuple-element.10), channel_id=1, source_target_pairs={{0,1},{1,2},{2,3},{3,0},{4,5},{5,6},{6,7},{7,4},{8,9},{9,10},{10,1... | collective-permute-start | bytes 2457608 | tf_op jit(solution)/shard_map/ppermute | solution.py:27
  41.1 0.0 collective-permute-done.4.refs_5_
  41.1 1.9 %collective-permute-start.7 = (bf16[400,1024]{1,0:T(8,128)(2,1)S(1)}, bf16[400,1024]{1,0:T(8,128)(2,1)S(1)}, u32[]{:S(2)}, u32[]{:S(2)}) collective-permute-start(bf16[400,1024]{1,0:T(8,128)(2,1)S(1)} %collective-permute-done.4.refs_5_), channel_id=1, source_target_pairs={{0,4},{1,5},{4,8},{5,9},{8,12},{9,13},{12,16},{13,17},{16,20},{17,... | collective-permute-start | bytes 2457608 | tf_op jit(solution)/shard_map/ppermute | solution.py:27
  43.0 14.5 %collective-permute-done.2.refs_3_ = bf16[400,1024]{1,0:T(8,128)(2,1)} collective-permute-done((bf16[400,1024]{1,0:T(8,128)(2,1)S(1)}, bf16[400,1024]{1,0:T(8,128)(2,1)}, u32[]{:S(2)}, u32[]{:S(2)}) %collective-permute-start.2) | collective-permute-done | bytes 819232 | tf_op jit(solution)/shard_map/ppermute | solution.py:27
  57.5 0.8 collective-permute-done.3.refs_4_
  58.2 6.8 %near.1 = (f32[384,1024]{1,0:T(8,128)S(1)}, f32[384,128]{1,0:T(8,128)S(1)}) custom-call(bf16[400,1024]{1,0:T(8,128)(2,1)S(1)} %pack.1.refs_0_, bf16[400,1024]{1,0:T(8,128)(2,1)S(1)} %collective-permute-done.refs_1_, bf16[400,1024]{1,0:T(8,128)(2,1)S(1)} %collective-permute-done.1.refs_2_, bf16[400,1024]{1,0:T(8,128)(2,1)} %collective-permute-done.2.refs_3_, ...), custom_call_target="tpu_custom_call" | custom-call | flops 3623878656 | bytes 5505024 | tf_op jit(solution)/shard_map/near/pallas_call | solution.py:122
  65.1 10.2 %collective-permute-done.5.refs_3_ = bf16[400,1024]{1,0:T(8,128)(2,1)S(1)} collective-permute-done((bf16[400,1024]{1,0:T(8,128)(2,1)S(1)}, bf16[400,1024]{1,0:T(8,128)(2,1)S(1)}, u32[]{:S(2)}, u32[]{:S(2)}) %collective-permute-start.5) | collective-permute-done | bytes 819232 | tf_op jit(solution)/shard_map/ppermute | solution.py:27
  75.2 0.0 collective-permute-done.6.refs_4_
  75.2 0.0 collective-permute-done.7.refs_5_
  75.2 4.0 %late.1 = (f32[384,1024]{1,0:T(8,128)}, f32[1,384]{1,0:T(1,128)S(1)}) custom-call(bf16[400,1024]{1,0:T(8,128)(2,1)S(1)} %pack.1.refs_0_, f32[384,1024]{1,0:T(8,128)S(1)} %get-tuple-element.6.refs_1_, f32[384,128]{1,0:T(8,128)S(1)} %get-tuple-element.7.refs_2_, bf16[400,1024]{1,0:T(8,128)(2,1)S(1)} %collective-permute-done.5.refs_3_, ...), custom_call_target="tpu_custom_call" | custom-call | flops 1811939328 | bytes 3145728 | tf_op jit(solution)/shard_map/late/pallas_call | solution.py:133
  79.2 0.6 reduce
Async XLA Ops:
  1.3 1.1 %copy-start = (bf16[384,1024]{1,0:T(8,128)(2,1)S(1)}, bf16[384,1024]{1,0:T(8,128)(2,1)}, u32[]{:S(2)}) copy-start(bf16[384,1024]{1,0:T(8,128)(2,1)} %values_ref.1) | copy-start | bytes 2359300
  2.7 29.1 %collective-permute-start = (bf16[400,1024]{1,0:T(8,128)(2,1)S(1)}, bf16[400,1024]{1,0:T(8,128)(2,1)S(1)}, u32[]{:S(2)}, u32[]{:S(2)}) collective-permute-start(bf16[400,1024]{1,0:T(8,128)(2,1)S(1)} %pack.1.refs_0_), channel_id=1, source_target_pairs={{0,4},{1,5},{2,6},{3,7},{4,8},{5,9},{6,10},{7,11},{8,12},{9,13},{1... | collective-permute-start | bytes 2457608 | tf_op jit(solution)/shard_map/ppermute | solution.py:27
  6.5 27.5 %collective-permute-start.1 = (bf16[400,1024]{1,0:T(8,128)(2,1)S(1)}, bf16[400,1024]{1,0:T(8,128)(2,1)S(1)}, u32[]{:S(2)}, u32[]{:S(2)}) collective-permute-start(bf16[400,1024]{1,0:T(8,128)(2,1)S(1)} %pack.1.refs_0_), channel_id=1, source_target_pairs={{4,0},{5,1},{6,2},{7,3},{8,4},{9,5},{10,6},{11,7},{12,8},{13,9},{1... | collective-permute-start | bytes 2457608 | tf_op jit(solution)/shard_map/ppermute | solution.py:27
  15.7 25.3 %collective-permute-start.4 = (bf16[400,1024]{1,0:T(8,128)(2,1)S(1)}, bf16[400,1024]{1,0:T(8,128)(2,1)S(1)}, u32[]{:S(2)}, u32[]{:S(2)}) collective-permute-start(bf16[400,1024]{1,0:T(8,128)(2,1)S(1)} %pack.1.refs_0_), channel_id=1, source_target_pairs={{0,2},{1,3},{2,0},{3,1},{4,6},{5,7},{6,4},{7,5},{8,10},{9,11},{10,... | collective-permute-start | bytes 2457608 | tf_op jit(solution)/shard_map/ppermute | solution.py:27
  20.9 36.6 %collective-permute-start.2 = (bf16[400,1024]{1,0:T(8,128)(2,1)S(1)}, bf16[400,1024]{1,0:T(8,128)(2,1)}, u32[]{:S(2)}, u32[]{:S(2)}) collective-permute-start(bf16[400,1024]{1,0:T(8,128)(2,1)S(1)} %pack.1.refs_0_), channel_id=1, source_target_pairs={{0,1},{1,2},{2,3},{3,0},{4,5},{5,6},{6,7},{7,4},{8,9},{9,10},{10,1... | collective-permute-start | bytes 2457608 | tf_op jit(solution)/shard_map/ppermute | solution.py:27
  23.4 34.8 %collective-permute-start.3 = (bf16[400,1024]{1,0:T(8,128)(2,1)S(1)}, bf16[400,1024]{1,0:T(8,128)(2,1)}, u32[]{:S(2)}, u32[]{:S(2)}) collective-permute-start(bf16[400,1024]{1,0:T(8,128)(2,1)S(1)} %pack.1.refs_0_), channel_id=1, source_target_pairs={{0,3},{1,0},{2,1},{3,2},{4,7},{5,4},{6,5},{7,6},{8,11},{9,8},{10,9... | collective-permute-start | bytes 2457608 | tf_op jit(solution)/shard_map/ppermute | solution.py:27
  34.2 41.0 %collective-permute-start.5 = (bf16[400,1024]{1,0:T(8,128)(2,1)S(1)}, bf16[400,1024]{1,0:T(8,128)(2,1)S(1)}, u32[]{:S(2)}, u32[]{:S(2)}) collective-permute-start(bf16[400,1024]{1,0:T(8,128)(2,1)S(1)} %get-tuple-element.11), channel_id=1, source_target_pairs={{0,3},{1,0},{2,1},{3,2},{4,7},{5,4},{6,5},{7,6},{8,11},{9,8},{10,9... | collective-permute-start | bytes 2457608 | tf_op jit(solution)/shard_map/ppermute | solution.py:27
  39.1 36.1 %collective-permute-start.6 = (bf16[400,1024]{1,0:T(8,128)(2,1)S(1)}, bf16[400,1024]{1,0:T(8,128)(2,1)S(1)}, u32[]{:S(2)}, u32[]{:S(2)}) collective-permute-start(bf16[400,1024]{1,0:T(8,128)(2,1)S(1)} %get-tuple-element.10), channel_id=1, source_target_pairs={{0,1},{1,2},{2,3},{3,0},{4,5},{5,6},{6,7},{7,4},{8,9},{9,10},{10,1... | collective-permute-start | bytes 2457608 | tf_op jit(solution)/shard_map/ppermute | solution.py:27
  41.1 34.2 %collective-permute-start.7 = (bf16[400,1024]{1,0:T(8,128)(2,1)S(1)}, bf16[400,1024]{1,0:T(8,128)(2,1)S(1)}, u32[]{:S(2)}, u32[]{:S(2)}) collective-permute-start(bf16[400,1024]{1,0:T(8,128)(2,1)S(1)} %collective-permute-done.4.refs_5_), channel_id=1, source_target_pairs={{0,4},{1,5},{4,8},{5,9},{8,12},{9,13},{12,16},{13,17},{16,20},{17,... | collective-permute-start | bytes 2457608 | tf_op jit(solution)/shard_map/ppermute | solution.py:27

commit v2 on v1

v2 whole, which is shorter than its diff:
```python
import functools
import math

import jax
import jax.numpy as jnp
from jax import lax
from jax.experimental import pallas as pl
from jax.experimental.pallas import tpu as pltpu
from jax.sharding import PartitionSpec as P

AXES = ("grp", "dev")
ROWS = 384
RING = 4
TAIL = 8
VMEM_BYTES = 40 * 1024 * 1024


def plane_pairs(total, up, along, columns=range(RING)):
    pairs = []
    for plane in range(total // RING):
        if 0 <= plane + up < total // RING:
            for column in columns:
                target = (column + along) % RING
                pairs.append((plane * RING + column, (plane + up) * RING + target))
    return pairs


def swaps(total, stride, start):
    pairs = []
    for low in range(start * stride, total - stride, 2 * stride):
        for device in range(low, low + stride):
            pairs += [(device, device + stride), (device + stride, device)]
    return pairs


def ring_swaps(total, start):
    pairs = []
    for plane in range(0, total, RING):
        for column in range(start, start + RING, 2):
            one, other = plane + column % RING, plane + (column + 1) % RING
            pairs += [(one, other), (other, one)]
    return pairs


def send(block, pairs):
    return lax.ppermute(block, AXES, pairs)


def pack_kernel(values_ref, label_ref, packed_ref):
    rows, width = values_ref.shape
    values = values_ref[...].astype(jnp.float32)
    scale = lax.rsqrt(jnp.mean(values * values, axis=1, keepdims=True) + 1e-06)
    packed_ref[:rows, :] = (values * scale).astype(jnp.bfloat16)
    label = (label_ref[...].reshape(1, rows) + 1).astype(jnp.float32).astype(jnp.bfloat16)
    packed_ref[rows:, :rows] = jnp.broadcast_to(label, (TAIL, rows))
    packed_ref[rows:, rows:] = jnp.zeros((TAIL, width - rows), jnp.bfloat16)


def labels_of(tail_ref):
    rows = tail_ref.shape[0] - TAIL
    return tail_ref[rows:, :ROWS].astype(jnp.float32)[:1, :]


def tile(own, own_label, far, far_label, kernel_scale, diagonal):
    scores = (
        lax.dot_general(own, far, (((1,), (1,)), ((), ())), preferred_element_type=jnp.float32)
        * kernel_scale
    )
    linked = own_label == far_label
    if diagonal:
        shape = scores.shape
        linked = linked & (
            lax.broadcasted_iota(jnp.int32, shape, 0) != lax.broadcasted_iota(jnp.int32, shape, 1)
        )
    weight = jnp.where(linked, jnp.exp(scores), 0.0)
    pull = jnp.dot(weight.astype(jnp.bfloat16), far, preferred_element_type=jnp.float32)
    return pull, jnp.sum(weight, axis=1, keepdims=True)


def block_kernel(kernel_scale, fresh, final, n_blocks, n_halves, own_ref, *refs):
    refs, (sum_ref, count_ref) = refs[:-2], refs[-2:]
    rows = own_ref.shape[0] - TAIL
    own = own_ref[:rows, :]
    own_row = labels_of(own_ref)
    own_label = jnp.broadcast_to(own_row, (128, rows)).T[:, :1]
    if fresh:
        pulled, counted = tile(own, own_label, own, own_row, kernel_scale, True)
    else:
        pulled, counted = refs[0][...], refs[1][:, :1]
        refs = refs[2:]
    parts = [(ref[:rows, :], labels_of(ref)) for ref in refs[:n_blocks]]
    for i in range(n_halves):
        top, bottom = refs[n_blocks + 2 * i], refs[n_blocks + 2 * i + 1]
        label, half = labels_of(bottom), top.shape[0]
        parts += [(top[...], label[:, :half]), (bottom[: rows - half, :], label[:, half:])]
    for far, far_label in parts:
        pull, count = tile(own, own_label, far, far_label, kernel_scale, False)
        pulled, counted = pulled + pull, counted + count
    if final:
        sum_ref[...] = pulled * (1.0 / (1.0 + counted))
        logs = jnp.log(1.0 + jnp.broadcast_to(counted, (rows, 128)).T[:1, :])
        count_ref[...] = logs.reshape(rows)
    else:
        sum_ref[...] = pulled
        count_ref[...] = jnp.broadcast_to(counted, count_ref.shape)


def cost(tiles, rows, width):
    return pl.CostEstimate(
        flops=4 * tiles * rows * rows * width,
        bytes_accessed=2 * (tiles + 1) * rows * width,
        transcendentals=tiles * rows * rows,
    )


def shards(embeddings, cluster_ids):
    rows, width = embeddings.shape
    total = lax.axis_size("grp") * lax.axis_size("dev")
    kernel_scale = 2.0 / math.sqrt(width)
    params = pltpu.CompilerParams(vmem_limit_bytes=VMEM_BYTES)
    block = jax.ShapeDtypeStruct((rows + TAIL, width), jnp.bfloat16)
    sums = jax.ShapeDtypeStruct((rows, width), jnp.float32)
    counts = jax.ShapeDtypeStruct((rows, 128), jnp.float32)
    own = pl.pallas_call(
        pack_kernel,
        out_shape=block,
        compiler_params=params,
        name="pack",
    )(embeddings, cluster_ids)
    column = lax.rem(lax.axis_index("dev"), RING)
    odd = lax.rem(lax.axis_index("dev") // RING, 2)

    def add(state, blocks, halves, final, name):
        return pl.pallas_call(
            functools.partial(block_kernel, kernel_scale, not state, final, len(blocks), len(halves) // 2),
            out_shape=(sums, jax.ShapeDtypeStruct((rows,), jnp.float32) if final else counts),
            compiler_params=params,
            cost_estimate=cost(len(blocks) + len(halves) // 2 + (not state), rows, width),
            name=name,
        )(own, *state, *blocks, *halves)

    across = send(own, plane_pairs(total, 0, 2))
    below = send(own, plane_pairs(total, 1, 0))
    above = send(own, plane_pairs(total, -1, 0))
    first_column = send(own, ring_swaps(total, 0))
    second_column = send(own, ring_swaps(total, 1))
    climb = plane_pairs(total, 1, 0, range(RING // 2)) + plane_pairs(
        total, -1, 0, range(RING // 2, RING)
    )
    corner = send(across, climb)
    first_side = send(jnp.where(lax.rem(column, 2) == 1, below, above), ring_swaps(total, 0))
    second_side = send(jnp.where(column >= RING // 2, below, above), ring_swaps(total, 1))
    state = add((), (across, above, below, first_column, second_column), (), False, "near")
    state = add(state, (corner,), (), False, "corner")
    state = add(state, (first_side,), (), False, "side")
    return add(state, (second_side,), (), True, "late")


def solution(mesh):
    placed = (P(AXES, None), P(AXES))
    return jax.shard_map(
        shards,
        mesh=mesh,
        in_specs=placed,
        out_specs=placed,
        check_vma=False,
    )
```

time: 80.2 us -> 66.9 us (0.83)
  waiting for transfers between devices: 31.5 us -> 19.8 us
  starting transfers between devices: 33.9 us -> 32.6 us
    ppermute x8, waiting for transfers between devices: 31.5 us -> 19.8 us  [send(): return lax.ppermute(block, AXES, pairs)]
    ppermute x8, starting transfers between devices: 33.9 us -> 32.6 us  [send(): return lax.ppermute(block, AXES, pairs)]
    unnamed x2 -> x4, local copies, waits for them, and re-layouts: 1.13 us -> 1.81 us
    pallas_call x3 -> x5, Pallas kernels: 11.1 us -> 11.4 us  [the longest x4 11.2 us: add(): pl.pallas_call(functools.partial(block_kernel, kernel_scale, not state, f...]
  transfers between devices with their start and end apart: 8 -> 8, of which waited for: 5 -> 7; matrix products, arithmetic and copies ran while one was open for 0% -> 0% of each run, Pallas kernels for 9% -> 13%
where the time goes in v2:
time: 66.9 us; the launch traced here: 66.5 us
  starting transfers between devices  32.6 us (49%)
  waiting for transfers between devices  19.8 us (30%)
  Pallas kernels  11.4 us (17%)
  local copies, waits for them, and re-layouts  1.81 us (3%)
  between operations  0.76 us (1%)
    ppermute x8, starting transfers between devices, send(): return lax.ppermute(block, AXES, pairs)  32.6 us
    ppermute x8, waiting for transfers between devices, send(): return lax.ppermute(block, AXES, pairs)  19.8 us
    pallas_call x4, Pallas kernels, add(): pl.pallas_call(functools.partial(block_kernel, kernel_scale, not state, f...  11.2 us
    unnamed x4, local copies, waits for them, and re-layouts  1.81 us
  transfers between devices with their start and end apart: 8, of which 7 were waited for; matrix products, arithmetic and copies ran while one was open for 0% of the time, Pallas kernels for 13%

profile of v2, /device:TPU:6, one launch (start us, length us, event | category | flops | bytes accessed | tf_op | source)
XLA Modules:
  0.0 66.5 jit_solution(487088337288955990)
XLA Ops:
  0.6 0.0 copy-start
  0.6 1.1 %copy-done = bf16[384,1024]{1,0:T(8,128)(2,1)S(1)} copy-done((bf16[384,1024]{1,0:T(8,128)(2,1)S(1)}, bf16[384,1024]{1,0:T(8,128)(2,1)}, u32[]{:S(2)}) %copy-start) | copy-done | bytes 786456
  1.8 0.0 copy-start.1
  1.8 0.7 %copy-done.1 = s32[384]{0:T(512)S(1)} copy-done((s32[384]{0:T(512)S(1)}, s32[384]{0:T(512)}, u32[]{:S(2)}) %copy-start.1) | copy-done | bytes 1560
  2.4 0.2 pack.1.own_ref
  2.7 5.1 %collective-permute-start = (bf16[392,1024]{1,0:T(8,128)(2,1)S(1)}, bf16[392,1024]{1,0:T(8,128)(2,1)S(1)}, u32[]{:S(2)}, u32[]{:S(2)}) collective-permute-start(bf16[392,1024]{1,0:T(8,128)(2,1)S(1)} %pack.1.own_ref), channel_id=1, source_target_pairs={{0,2},{1,3},{2,0},{3,1},{4,6},{5,7},{6,4},{7,5},{8,10},{9,11},{10,... | collective-permute-start | bytes 2408456 | tf_op jit(solution)/shard_map/ppermute | solution.py:46
  7.8 3.8 %collective-permute-start.2 = (bf16[392,1024]{1,0:T(8,128)(2,1)S(1)}, bf16[392,1024]{1,0:T(8,128)(2,1)S(1)}, u32[]{:S(2)}, u32[]{:S(2)}) collective-permute-start(bf16[392,1024]{1,0:T(8,128)(2,1)S(1)} %pack.1.own_ref), channel_id=1, source_target_pairs={{0,4},{1,5},{2,6},{3,7},{4,8},{5,9},{6,10},{7,11},{8,12},{9,13},{1... | collective-permute-start | bytes 2408456 | tf_op jit(solution)/shard_map/ppermute | solution.py:46
  11.6 8.9 %collective-permute-start.1 = (bf16[392,1024]{1,0:T(8,128)(2,1)S(1)}, bf16[392,1024]{1,0:T(8,128)(2,1)S(1)}, u32[]{:S(2)}, u32[]{:S(2)}) collective-permute-start(bf16[392,1024]{1,0:T(8,128)(2,1)S(1)} %pack.1.own_ref), channel_id=1, source_target_pairs={{4,0},{5,1},{6,2},{7,3},{8,4},{9,5},{10,6},{11,7},{12,8},{13,9},{1... | collective-permute-start | bytes 2408456 | tf_op jit(solution)/shard_map/ppermute | solution.py:46
  20.6 3.0 %collective-permute-start.4 = (bf16[392,1024]{1,0:T(8,128)(2,1)S(1)}, bf16[392,1024]{1,0:T(8,128)(2,1)}, u32[]{:S(2)}, u32[]{:S(2)}) collective-permute-start(bf16[392,1024]{1,0:T(8,128)(2,1)S(1)} %pack.1.own_ref), channel_id=1, source_target_pairs={{1,2},{2,1},{3,0},{0,3},{5,6},{6,5},{7,4},{4,7},{9,10},{10,9},{11,... | collective-permute-start | bytes 2408456 | tf_op jit(solution)/shard_map/ppermute | solution.py:46
  23.5 1.9 %collective-permute-start.3 = (bf16[392,1024]{1,0:T(8,128)(2,1)S(1)}, bf16[392,1024]{1,0:T(8,128)(2,1)}, u32[]{:S(2)}, u32[]{:S(2)}) collective-permute-start(bf16[392,1024]{1,0:T(8,128)(2,1)S(1)} %pack.1.own_ref), channel_id=1, source_target_pairs={{0,1},{1,0},{2,3},{3,2},{4,5},{5,4},{6,7},{7,6},{8,9},{9,8},{10,11... | collective-permute-start | bytes 2408456 | tf_op jit(solution)/shard_map/ppermute | solution.py:46
  25.5 0.2 collective-permute-done.refs_0_
  25.7 5.0 %collective-permute-start.5 = (bf16[392,1024]{1,0:T(8,128)(2,1)S(1)}, bf16[392,1024]{1,0:T(8,128)(2,1)S(1)}, u32[]{:S(2)}, u32[]{:S(2)}) collective-permute-start(bf16[392,1024]{1,0:T(8,128)(2,1)S(1)} %collective-permute-done.refs_0_), channel_id=1, source_target_pairs={{0,4},{1,5},{4,8},{5,9},{8,12},{9,13},{12,16},{13,17},{16,20},{17,... | collective-permute-start | bytes 2408456 | tf_op jit(solution)/shard_map/ppermute | solution.py:46
  30.7 5.2 %collective-permute-done.2.refs_2_ = bf16[392,1024]{1,0:T(8,128)(2,1)S(1)} collective-permute-done((bf16[392,1024]{1,0:T(8,128)(2,1)S(1)}, bf16[392,1024]{1,0:T(8,128)(2,1)S(1)}, u32[]{:S(2)}, u32[]{:S(2)}) %collective-permute-start.2) | collective-permute-done | bytes 802848 | tf_op jit(solution)/shard_map/ppermute | solution.py:46
  35.9 2.9 %collective-permute-done.1.refs_1_ = bf16[392,1024]{1,0:T(8,128)(2,1)S(1)} collective-permute-done((bf16[392,1024]{1,0:T(8,128)(2,1)S(1)}, bf16[392,1024]{1,0:T(8,128)(2,1)S(1)}, u32[]{:S(2)}, u32[]{:S(2)}) %collective-permute-start.1) | collective-permute-done | bytes 802848 | tf_op jit(solution)/shard_map/ppermute | solution.py:46
  38.8 0.1 broadcast_select_fusion
  38.9 2.6 %collective-permute-start.6 = (bf16[392,1024]{1,0:T(8,128)(2,1)S(1)}, bf16[392,1024]{1,0:T(8,128)(2,1)S(1)}, u32[]{:S(2)}, u32[]{:S(2)}) collective-permute-start(bf16[392,1024]{1,0:T(8,128)(2,1)S(1)} %get-tuple-element.15), channel_id=1, source_target_pairs={{0,1},{1,0},{2,3},{3,2},{4,5},{5,4},{6,7},{7,6},{8,9},{9,8},{10,11... | collective-permute-start | bytes 2408456 | tf_op jit(solution)/shard_map/ppermute | solution.py:46
  41.5 2.3 %collective-permute-start.7 = (bf16[392,1024]{1,0:T(8,128)(2,1)S(1)}, bf16[392,1024]{1,0:T(8,128)(2,1)S(1)}, u32[]{:S(2)}, u32[]{:S(2)}) collective-permute-start(bf16[392,1024]{1,0:T(8,128)(2,1)S(1)} %get-tuple-element.14), channel_id=1, source_target_pairs={{1,2},{2,1},{3,0},{0,3},{5,6},{6,5},{7,4},{4,7},{9,10},{10,9},{11,... | collective-permute-start | bytes 2408456 | tf_op jit(solution)/shard_map/ppermute | solution.py:46
  43.8 0.4 collective-permute-done.4.refs_4_
  44.3 2.0 %collective-permute-done.3.refs_3_ = bf16[392,1024]{1,0:T(8,128)(2,1)} collective-permute-done((bf16[392,1024]{1,0:T(8,128)(2,1)S(1)}, bf16[392,1024]{1,0:T(8,128)(2,1)}, u32[]{:S(2)}, u32[]{:S(2)}) %collective-permute-start.3) | collective-permute-done | bytes 802848 | tf_op jit(solution)/shard_map/ppermute | solution.py:46
  46.2 6.8 %near.1 = (f32[384,1024]{1,0:T(8,128)S(1)}, f32[384,128]{1,0:T(8,128)S(1)}) custom-call(bf16[392,1024]{1,0:T(8,128)(2,1)S(1)} %pack.1.own_ref, bf16[392,1024]{1,0:T(8,128)(2,1)S(1)} %collective-permute-done.refs_0_, bf16[392,1024]{1,0:T(8,128)(2,1)S(1)} %collective-permute-done.1.refs_1_, bf16[392,1024]{1,0:T(8,128)(2,1)S(1)} %collective-permute-done.2.refs_2_, ...), custom_call_target="tpu_custom_call" | custom-call | flops 3623878656 | bytes 5505024 | tf_op jit(solution)/shard_map/near/pallas_call | solution.py:134
  53.1 0.0 collective-permute-done.5.refs_2_
  53.1 1.1 %corner.1 = (f32[384,1024]{1,0:T(8,128)S(1)}, f32[384,128]{1,0:T(8,128)S(1)}) custom-call(bf16[392,1024]{1,0:T(8,128)(2,1)S(1)} %pack.1.own_ref, f32[384,1024]{1,0:T(8,128)S(1)} %get-tuple-element.8.refs_0_, f32[384,128]{1,0:T(8,128)S(1)} %get-tuple-element.9.refs_1_, bf16[392,1024]{1,0:T(8,128)(2,1)S(1)} %collective-permute-done.5.refs_2_), custom_call_target="tpu_custom_call" | custom-call | flops 603979776 | bytes 1572864 | tf_op jit(solution)/shard_map/corner/pallas_call | solution.py:134
  54.2 8.7 %collective-permute-done.6.refs_2_ = bf16[392,1024]{1,0:T(8,128)(2,1)S(1)} collective-permute-done((bf16[392,1024]{1,0:T(8,128)(2,1)S(1)}, bf16[392,1024]{1,0:T(8,128)(2,1)S(1)}, u32[]{:S(2)}, u32[]{:S(2)}) %collective-permute-start.6) | collective-permute-done | bytes 802848 | tf_op jit(solution)/shard_map/ppermute | solution.py:46
  62.9 1.1 %side.1 = (f32[384,1024]{1,0:T(8,128)S(1)}, f32[384,128]{1,0:T(8,128)S(1)}) custom-call(bf16[392,1024]{1,0:T(8,128)(2,1)S(1)} %pack.1.own_ref, f32[384,1024]{1,0:T(8,128)S(1)} %get-tuple-element.10.refs_0_, f32[384,128]{1,0:T(8,128)S(1)} %get-tuple-element.11.refs_1_, bf16[392,1024]{1,0:T(8,128)(2,1)S(1)} %collective-permute-done.6.refs_2_), custom_call_target="tpu_custom_call" | custom-call | flops 603979776 | bytes 1572864 | tf_op jit(solution)/shard_map/side/pallas_call | solution.py:134
  64.0 0.3 collective-permute-done.7.refs_2_
  64.3 2.2 %late.1 = (f32[384,1024]{1,0:T(8,128)}, f32[384]{0:T(512)}) custom-call(bf16[392,1024]{1,0:T(8,128)(2,1)S(1)} %pack.1.own_ref, f32[384,1024]{1,0:T(8,128)S(1)} %get-tuple-element.12.refs_0_, f32[384,128]{1,0:T(8,128)S(1)} %get-tuple-element.13.refs_1_, bf16[392,1024]{1,0:T(8,128)(2,1)S(1)} %collective-permute-done.7.refs_2_), custom_call_target="tpu_custom_call" | custom-call | flops 603979776 | bytes 1572864 | tf_op jit(solution)/shard_map/late/pallas_call | solution.py:134
Async XLA Ops:
  0.6 1.1 %copy-start = (bf16[384,1024]{1,0:T(8,128)(2,1)S(1)}, bf16[384,1024]{1,0:T(8,128)(2,1)}, u32[]{:S(2)}) copy-start(bf16[384,1024]{1,0:T(8,128)(2,1)} %values_ref.1) | copy-start | bytes 2359300
  1.8 0.7 %copy-start.1 = (s32[384]{0:T(512)S(1)}, s32[384]{0:T(512)}, u32[]{:S(2)}) copy-start(s32[384]{0:T(512)} %label_ref.1) | copy-start | bytes 4612
  2.7 23.0 %collective-permute-start = (bf16[392,1024]{1,0:T(8,128)(2,1)S(1)}, bf16[392,1024]{1,0:T(8,128)(2,1)S(1)}, u32[]{:S(2)}, u32[]{:S(2)}) collective-permute-start(bf16[392,1024]{1,0:T(8,128)(2,1)S(1)} %pack.1.own_ref), channel_id=1, source_target_pairs={{0,2},{1,3},{2,0},{3,1},{4,6},{5,7},{6,4},{7,5},{8,10},{9,11},{10,... | collective-permute-start | bytes 2408456 | tf_op jit(solution)/shard_map/ppermute | solution.py:46
  7.8 28.1 %collective-permute-start.2 = (bf16[392,1024]{1,0:T(8,128)(2,1)S(1)}, bf16[392,1024]{1,0:T(8,128)(2,1)S(1)}, u32[]{:S(2)}, u32[]{:S(2)}) collective-permute-start(bf16[392,1024]{1,0:T(8,128)(2,1)S(1)} %pack.1.own_ref), channel_id=1, source_target_pairs={{0,4},{1,5},{2,6},{3,7},{4,8},{5,9},{6,10},{7,11},{8,12},{9,13},{1... | collective-permute-start | bytes 2408456 | tf_op jit(solution)/shard_map/ppermute | solution.py:46
  11.6 27.2 %collective-permute-start.1 = (bf16[392,1024]{1,0:T(8,128)(2,1)S(1)}, bf16[392,1024]{1,0:T(8,128)(2,1)S(1)}, u32[]{:S(2)}, u32[]{:S(2)}) collective-permute-start(bf16[392,1024]{1,0:T(8,128)(2,1)S(1)} %pack.1.own_ref), channel_id=1, source_target_pairs={{4,0},{5,1},{6,2},{7,3},{8,4},{9,5},{10,6},{11,7},{12,8},{13,9},{1... | collective-permute-start | bytes 2408456 | tf_op jit(solution)/shard_map/ppermute | solution.py:46
  20.6 23.7 %collective-permute-start.4 = (bf16[392,1024]{1,0:T(8,128)(2,1)S(1)}, bf16[392,1024]{1,0:T(8,128)(2,1)}, u32[]{:S(2)}, u32[]{:S(2)}) collective-permute-start(bf16[392,1024]{1,0:T(8,128)(2,1)S(1)} %pack.1.own_ref), channel_id=1, source_target_pairs={{1,2},{2,1},{3,0},{0,3},{5,6},{6,5},{7,4},{4,7},{9,10},{10,9},{11,... | collective-permute-start | bytes 2408456 | tf_op jit(solution)/shard_map/ppermute | solution.py:46
  23.5 22.7 %collective-permute-start.3 = (bf16[392,1024]{1,0:T(8,128)(2,1)S(1)}, bf16[392,1024]{1,0:T(8,128)(2,1)}, u32[]{:S(2)}, u32[]{:S(2)}) collective-permute-start(bf16[392,1024]{1,0:T(8,128)(2,1)S(1)} %pack.1.own_ref), channel_id=1, source_target_pairs={{0,1},{1,0},{2,3},{3,2},{4,5},{5,4},{6,7},{7,6},{8,9},{9,8},{10,11... | collective-permute-start | bytes 2408456 | tf_op jit(solution)/shard_map/ppermute | solution.py:46
  25.7 27.3 %collective-permute-start.5 = (bf16[392,1024]{1,0:T(8,128)(2,1)S(1)}, bf16[392,1024]{1,0:T(8,128)(2,1)S(1)}, u32[]{:S(2)}, u32[]{:S(2)}) collective-permute-start(bf16[392,1024]{1,0:T(8,128)(2,1)S(1)} %collective-permute-done.refs_0_), channel_id=1, source_target_pairs={{0,4},{1,5},{4,8},{5,9},{8,12},{9,13},{12,16},{13,17},{16,20},{17,... | collective-permute-start | bytes 2408456 | tf_op jit(solution)/shard_map/ppermute | solution.py:46
  38.9 23.9 %collective-permute-start.6 = (bf16[392,1024]{1,0:T(8,128)(2,1)S(1)}, bf16[392,1024]{1,0:T(8,128)(2,1)S(1)}, u32[]{:S(2)}, u32[]{:S(2)}) collective-permute-start(bf16[392,1024]{1,0:T(8,128)(2,1)S(1)} %get-tuple-element.15), channel_id=1, source_target_pairs={{0,1},{1,0},{2,3},{3,2},{4,5},{5,4},{6,7},{7,6},{8,9},{9,8},{10,11... | collective-permute-start | bytes 2408456 | tf_op jit(solution)/shard_map/ppermute | solution.py:46
  41.5 22.7 %collective-permute-start.7 = (bf16[392,1024]{1,0:T(8,128)(2,1)S(1)}, bf16[392,1024]{1,0:T(8,128)(2,1)S(1)}, u32[]{:S(2)}, u32[]{:S(2)}) collective-permute-start(bf16[392,1024]{1,0:T(8,128)(2,1)S(1)} %get-tuple-element.14), channel_id=1, source_target_pairs={{1,2},{2,1},{3,0},{0,3},{5,6},{6,5},{7,4},{4,7},{9,10},{10,9},{11,... | collective-permute-start | bytes 2408456 | tf_op jit(solution)/shard_map/ppermute | solution.py:46

commit v3 on v2

--- a/solution.py
+++ b/solution.py
@@ -11,6 +11,7 @@
 AXES = ("grp", "dev")
 ROWS = 384
 RING = 4
+CHUNKS = 2
 TAIL = 8
 VMEM_BYTES = 40 * 1024 * 1024
 
@@ -46,14 +47,26 @@
     return lax.ppermute(block, AXES, pairs)
 
 
-def pack_kernel(values_ref, label_ref, packed_ref):
+def pack_kernel(values_hbm, label_hbm, packed_ref, values_ref, label_ref, semaphores):
     rows, width = values_ref.shape
-    values = values_ref[...].astype(jnp.float32)
-    scale = lax.rsqrt(jnp.mean(values * values, axis=1, keepdims=True) + 1e-06)
-    packed_ref[:rows, :] = (values * scale).astype(jnp.bfloat16)
+    label_copy = pltpu.make_async_copy(label_hbm, label_ref, semaphores.at[CHUNKS])
+    chunks = [pl.ds(i * (rows // CHUNKS), rows // CHUNKS) for i in range(CHUNKS)]
+    copies = [
+        pltpu.make_async_copy(values_hbm.at[chunk], values_ref.at[chunk], semaphores.at[i])
+        for i, chunk in enumerate(chunks)
+    ]
+    label_copy.start()
+    for copy in copies:
+        copy.start()
+    packed_ref[rows:, rows:] = jnp.zeros((TAIL, width - rows), jnp.bfloat16)
+    label_copy.wait()
     label = (label_ref[...].reshape(1, rows) + 1).astype(jnp.float32).astype(jnp.bfloat16)
     packed_ref[rows:, :rows] = jnp.broadcast_to(label, (TAIL, rows))
-    packed_ref[rows:, rows:] = jnp.zeros((TAIL, width - rows), jnp.bfloat16)
+    for copy, chunk in zip(copies, chunks):
+        copy.wait()
+        values = values_ref[chunk, :].astype(jnp.float32)
+        scale = lax.rsqrt(jnp.mean(values * values, axis=1, keepdims=True) + 1e-06)
+        packed_ref[chunk, :] = (values * scale).astype(jnp.bfloat16)
 
 
 def labels_of(tail_ref):
@@ -124,9 +137,18 @@
     own = pl.pallas_call(
         pack_kernel,
         out_shape=block,
+        in_specs=[pl.BlockSpec(memory_space=pl.ANY)] * 2,
+        scratch_shapes=[
+            pltpu.VMEM((rows, width), jnp.bfloat16),
+            pltpu.VMEM((rows,), jnp.int32),
+            pltpu.SemaphoreType.DMA((CHUNKS + 1,)),
+        ],
         compiler_params=params,
         name="pack",
-    )(embeddings, cluster_ids)
+    )(
+        pltpu.with_memory_space_constraint(embeddings, pltpu.HBM),
+        pltpu.with_memory_space_constraint(cluster_ids, pltpu.HBM),
+    )
     column = lax.rem(lax.axis_index("dev"), RING)
     odd = lax.rem(lax.axis_index("dev") // RING, 2)
 
@@ -150,7 +172,7 @@
     corner = send(across, climb)
     first_side = send(jnp.where(lax.rem(column, 2) == 1, below, above), ring_swaps(total, 0))
     second_side = send(jnp.where(column >= RING // 2, below, above), ring_swaps(total, 1))
-    state = add((), (across, above, below, first_column, second_column), (), False, "near")
+    state = add((), (across, above, below, second_column, first_column), (), False, "near")
     state = add(state, (corner,), (), False, "corner")
     state = add(state, (first_side,), (), False, "side")
     return add(state, (second_side,), (), True, "late")

time: 66.9 us -> 66.2 us (0.990)
  local copies, waits for them, and re-layouts: 1.81 us -> 0 us
  Pallas kernels: 11.4 us -> 12.6 us
    unnamed x4 -> x0, local copies, waits for them, and re-layouts: 1.81 us -> none
    pallas_call x1, Pallas kernels: 0.25 us -> 1.37 us  [shards(): pl.pallas_call(pack_kernel, out_shape=block, in_specs=[pl.BlockSpec(memor...]
  transfers between devices with their start and end apart: 8 -> 8, of which waited for: 7 -> 6; matrix products, arithmetic and copies ran while one was open for 0% -> 0% of each run, Pallas kernels for 13% -> 14%
where the time goes in v3:
time: 66.2 us; the launch traced here: 65.8 us
  starting transfers between devices  32.5 us (49%)
  waiting for transfers between devices  19.9 us (30%)
  Pallas kernels  12.6 us (19%)
  between operations  0.76 us (1%)
    ppermute x8, starting transfers between devices, send(): return lax.ppermute(block, AXES, pairs)  32.5 us
    ppermute x8, waiting for transfers between devices, send(): return lax.ppermute(block, AXES, pairs)  19.9 us
    pallas_call x4, Pallas kernels, add(): pl.pallas_call(functools.partial(block_kernel, kernel_scale, not state, f...  11.2 us
    pallas_call x1, Pallas kernels, shards(): pl.pallas_call(pack_kernel, out_shape=block, in_specs=[pl.BlockSpec(memor...  1.37 us
  transfers between devices with their start and end apart: 8, of which 6 were waited for; matrix products, arithmetic and copies ran while one was open for 0% of the time, Pallas kernels for 14%

profile of v3, /device:TPU:6, one launch (start us, length us, event | category | flops | bytes accessed | tf_op | source)
XLA Modules:
  0.0 65.8 jit_solution(6990346700477135697)
XLA Ops:
  0.6 1.4 %pack.1.own_ref = bf16[392,1024]{1,0:T(8,128)(2,1)S(1)} custom-call(bf16[384,1024]{1,0:T(8,128)(2,1)} %values_hbm.1, s32[384]{0:T(512)} %label_hbm.1), custom_call_target="tpu_custom_call" | custom-call | tf_op jit(solution)/shard_map/pack/pallas_call | solution.py:137
  2.0 5.1 %collective-permute-start = (bf16[392,1024]{1,0:T(8,128)(2,1)S(1)}, bf16[392,1024]{1,0:T(8,128)(2,1)S(1)}, u32[]{:S(2)}, u32[]{:S(2)}) collective-permute-start(bf16[392,1024]{1,0:T(8,128)(2,1)S(1)} %pack.1.own_ref), channel_id=1, source_target_pairs={{0,2},{1,3},{2,0},{3,1},{4,6},{5,7},{6,4},{7,5},{8,10},{9,11},{10,... | collective-permute-start | bytes 2408456 | tf_op jit(solution)/shard_map/ppermute | solution.py:47
  7.1 3.8 %collective-permute-start.2 = (bf16[392,1024]{1,0:T(8,128)(2,1)S(1)}, bf16[392,1024]{1,0:T(8,128)(2,1)S(1)}, u32[]{:S(2)}, u32[]{:S(2)}) collective-permute-start(bf16[392,1024]{1,0:T(8,128)(2,1)S(1)} %pack.1.own_ref), channel_id=1, source_target_pairs={{0,4},{1,5},{2,6},{3,7},{4,8},{5,9},{6,10},{7,11},{8,12},{9,13},{1... | collective-permute-start | bytes 2408456 | tf_op jit(solution)/shard_map/ppermute | solution.py:47
  10.9 8.9 %collective-permute-start.1 = (bf16[392,1024]{1,0:T(8,128)(2,1)S(1)}, bf16[392,1024]{1,0:T(8,128)(2,1)S(1)}, u32[]{:S(2)}, u32[]{:S(2)}) collective-permute-start(bf16[392,1024]{1,0:T(8,128)(2,1)S(1)} %pack.1.own_ref), channel_id=1, source_target_pairs={{4,0},{5,1},{6,2},{7,3},{8,4},{9,5},{10,6},{11,7},{12,8},{13,9},{1... | collective-permute-start | bytes 2408456 | tf_op jit(solution)/shard_map/ppermute | solution.py:47
  19.9 2.6 %collective-permute-start.4 = (bf16[392,1024]{1,0:T(8,128)(2,1)S(1)}, bf16[392,1024]{1,0:T(8,128)(2,1)}, u32[]{:S(2)}, u32[]{:S(2)}) collective-permute-start(bf16[392,1024]{1,0:T(8,128)(2,1)S(1)} %pack.1.own_ref), channel_id=1, source_target_pairs={{0,1},{1,0},{2,3},{3,2},{4,5},{5,4},{6,7},{7,6},{8,9},{9,8},{10,11... | collective-permute-start | bytes 2408456 | tf_op jit(solution)/shard_map/ppermute | solution.py:47
  22.5 2.3 %collective-permute-start.3 = (bf16[392,1024]{1,0:T(8,128)(2,1)S(1)}, bf16[392,1024]{1,0:T(8,128)(2,1)}, u32[]{:S(2)}, u32[]{:S(2)}) collective-permute-start(bf16[392,1024]{1,0:T(8,128)(2,1)S(1)} %pack.1.own_ref), channel_id=1, source_target_pairs={{1,2},{2,1},{3,0},{0,3},{5,6},{6,5},{7,4},{4,7},{9,10},{10,9},{11,... | collective-permute-start | bytes 2408456 | tf_op jit(solution)/shard_map/ppermute | solution.py:47
  24.8 0.4 collective-permute-done.refs_0_
  25.2 4.9 %collective-permute-start.5 = (bf16[392,1024]{1,0:T(8,128)(2,1)S(1)}, bf16[392,1024]{1,0:T(8,128)(2,1)S(1)}, u32[]{:S(2)}, u32[]{:S(2)}) collective-permute-start(bf16[392,1024]{1,0:T(8,128)(2,1)S(1)} %collective-permute-done.refs_0_), channel_id=1, source_target_pairs={{0,4},{1,5},{4,8},{5,9},{8,12},{9,13},{12,16},{13,17},{16,20},{17,... | collective-permute-start | bytes 2408456 | tf_op jit(solution)/shard_map/ppermute | solution.py:47
  30.0 5.2 %collective-permute-done.2.refs_2_ = bf16[392,1024]{1,0:T(8,128)(2,1)S(1)} collective-permute-done((bf16[392,1024]{1,0:T(8,128)(2,1)S(1)}, bf16[392,1024]{1,0:T(8,128)(2,1)S(1)}, u32[]{:S(2)}, u32[]{:S(2)}) %collective-permute-start.2) | collective-permute-done | bytes 802848 | tf_op jit(solution)/shard_map/ppermute | solution.py:47
  35.2 2.9 %collective-permute-done.1.refs_1_ = bf16[392,1024]{1,0:T(8,128)(2,1)S(1)} collective-permute-done((bf16[392,1024]{1,0:T(8,128)(2,1)S(1)}, bf16[392,1024]{1,0:T(8,128)(2,1)S(1)}, u32[]{:S(2)}, u32[]{:S(2)}) %collective-permute-start.1) | collective-permute-done | bytes 802848 | tf_op jit(solution)/shard_map/ppermute | solution.py:47
  38.1 0.1 broadcast_select_fusion
  38.3 2.6 %collective-permute-start.6 = (bf16[392,1024]{1,0:T(8,128)(2,1)S(1)}, bf16[392,1024]{1,0:T(8,128)(2,1)S(1)}, u32[]{:S(2)}, u32[]{:S(2)}) collective-permute-start(bf16[392,1024]{1,0:T(8,128)(2,1)S(1)} %get-tuple-element.15), channel_id=1, source_target_pairs={{0,1},{1,0},{2,3},{3,2},{4,5},{5,4},{6,7},{7,6},{8,9},{9,8},{10,11... | collective-permute-start | bytes 2408456 | tf_op jit(solution)/shard_map/ppermute | solution.py:47
  40.8 2.3 %collective-permute-start.7 = (bf16[392,1024]{1,0:T(8,128)(2,1)S(1)}, bf16[392,1024]{1,0:T(8,128)(2,1)S(1)}, u32[]{:S(2)}, u32[]{:S(2)}) collective-permute-start(bf16[392,1024]{1,0:T(8,128)(2,1)S(1)} %get-tuple-element.14), channel_id=1, source_target_pairs={{1,2},{2,1},{3,0},{0,3},{5,6},{6,5},{7,4},{4,7},{9,10},{10,9},{11,... | collective-permute-start | bytes 2408456 | tf_op jit(solution)/shard_map/ppermute | solution.py:47
  43.1 0.0 collective-permute-done.4.refs_4_
  43.2 2.8 %collective-permute-done.3.refs_3_ = bf16[392,1024]{1,0:T(8,128)(2,1)} collective-permute-done((bf16[392,1024]{1,0:T(8,128)(2,1)S(1)}, bf16[392,1024]{1,0:T(8,128)(2,1)}, u32[]{:S(2)}, u32[]{:S(2)}) %collective-permute-start.3) | collective-permute-done | bytes 802848 | tf_op jit(solution)/shard_map/ppermute | solution.py:47
  45.9 6.8 %near.1 = (f32[384,1024]{1,0:T(8,128)S(1)}, f32[384,128]{1,0:T(8,128)S(1)}) custom-call(bf16[392,1024]{1,0:T(8,128)(2,1)S(1)} %pack.1.own_ref, bf16[392,1024]{1,0:T(8,128)(2,1)S(1)} %collective-permute-done.refs_0_, bf16[392,1024]{1,0:T(8,128)(2,1)S(1)} %collective-permute-done.1.refs_1_, bf16[392,1024]{1,0:T(8,128)(2,1)S(1)} %collective-permute-done.2.refs_2_, ...), custom_call_target="tpu_custom_call" | custom-call | flops 3623878656 | bytes 5505024 | tf_op jit(solution)/shard_map/near/pallas_call | solution.py:156
  52.7 0.0 collective-permute-done.5.refs_2_
  52.7 1.1 %corner.1 = (f32[384,1024]{1,0:T(8,128)S(1)}, f32[384,128]{1,0:T(8,128)S(1)}) custom-call(bf16[392,1024]{1,0:T(8,128)(2,1)S(1)} %pack.1.own_ref, f32[384,1024]{1,0:T(8,128)S(1)} %get-tuple-element.8.refs_0_, f32[384,128]{1,0:T(8,128)S(1)} %get-tuple-element.9.refs_1_, bf16[392,1024]{1,0:T(8,128)(2,1)S(1)} %collective-permute-done.5.refs_2_), custom_call_target="tpu_custom_call" | custom-call | flops 603979776 | bytes 1572864 | tf_op jit(solution)/shard_map/corner/pallas_call | solution.py:156
  53.8 6.2 %collective-permute-done.6.refs_2_ = bf16[392,1024]{1,0:T(8,128)(2,1)S(1)} collective-permute-done((bf16[392,1024]{1,0:T(8,128)(2,1)S(1)}, bf16[392,1024]{1,0:T(8,128)(2,1)S(1)}, u32[]{:S(2)}, u32[]{:S(2)}) %collective-permute-start.6) | collective-permute-done | bytes 802848 | tf_op jit(solution)/shard_map/ppermute | solution.py:47
  60.1 1.1 %side.1 = (f32[384,1024]{1,0:T(8,128)S(1)}, f32[384,128]{1,0:T(8,128)S(1)}) custom-call(bf16[392,1024]{1,0:T(8,128)(2,1)S(1)} %pack.1.own_ref, f32[384,1024]{1,0:T(8,128)S(1)} %get-tuple-element.10.refs_0_, f32[384,128]{1,0:T(8,128)S(1)} %get-tuple-element.11.refs_1_, bf16[392,1024]{1,0:T(8,128)(2,1)S(1)} %collective-permute-done.6.refs_2_), custom_call_target="tpu_custom_call" | custom-call | flops 603979776 | bytes 1572864 | tf_op jit(solution)/shard_map/side/pallas_call | solution.py:156
  61.1 2.4 %collective-permute-done.7.refs_2_ = bf16[392,1024]{1,0:T(8,128)(2,1)S(1)} collective-permute-done((bf16[392,1024]{1,0:T(8,128)(2,1)S(1)}, bf16[392,1024]{1,0:T(8,128)(2,1)S(1)}, u32[]{:S(2)}, u32[]{:S(2)}) %collective-permute-start.7) | collective-permute-done | bytes 802848 | tf_op jit(solution)/shard_map/ppermute | solution.py:47
  63.6 2.2 %late.1 = (f32[384,1024]{1,0:T(8,128)}, f32[384]{0:T(512)}) custom-call(bf16[392,1024]{1,0:T(8,128)(2,1)S(1)} %pack.1.own_ref, f32[384,1024]{1,0:T(8,128)S(1)} %get-tuple-element.12.refs_0_, f32[384,128]{1,0:T(8,128)S(1)} %get-tuple-element.13.refs_1_, bf16[392,1024]{1,0:T(8,128)(2,1)S(1)} %collective-permute-done.7.refs_2_), custom_call_target="tpu_custom_call" | custom-call | flops 603979776 | bytes 1572864 | tf_op jit(solution)/shard_map/late/pallas_call | solution.py:156
Async XLA Ops:
  2.0 23.2 %collective-permute-start = (bf16[392,1024]{1,0:T(8,128)(2,1)S(1)}, bf16[392,1024]{1,0:T(8,128)(2,1)S(1)}, u32[]{:S(2)}, u32[]{:S(2)}) collective-permute-start(bf16[392,1024]{1,0:T(8,128)(2,1)S(1)} %pack.1.own_ref), channel_id=1, source_target_pairs={{0,2},{1,3},{2,0},{3,1},{4,6},{5,7},{6,4},{7,5},{8,10},{9,11},{10,... | collective-permute-start | bytes 2408456 | tf_op jit(solution)/shard_map/ppermute | solution.py:47
  7.1 28.1 %collective-permute-start.2 = (bf16[392,1024]{1,0:T(8,128)(2,1)S(1)}, bf16[392,1024]{1,0:T(8,128)(2,1)S(1)}, u32[]{:S(2)}, u32[]{:S(2)}) collective-permute-start(bf16[392,1024]{1,0:T(8,128)(2,1)S(1)} %pack.1.own_ref), channel_id=1, source_target_pairs={{0,4},{1,5},{2,6},{3,7},{4,8},{5,9},{6,10},{7,11},{8,12},{9,13},{1... | collective-permute-start | bytes 2408456 | tf_op jit(solution)/shard_map/ppermute | solution.py:47
  10.9 27.2 %collective-permute-start.1 = (bf16[392,1024]{1,0:T(8,128)(2,1)S(1)}, bf16[392,1024]{1,0:T(8,128)(2,1)S(1)}, u32[]{:S(2)}, u32[]{:S(2)}) collective-permute-start(bf16[392,1024]{1,0:T(8,128)(2,1)S(1)} %pack.1.own_ref), channel_id=1, source_target_pairs={{4,0},{5,1},{6,2},{7,3},{8,4},{9,5},{10,6},{11,7},{12,8},{13,9},{1... | collective-permute-start | bytes 2408456 | tf_op jit(solution)/shard_map/ppermute | solution.py:47
  19.9 23.3 %collective-permute-start.4 = (bf16[392,1024]{1,0:T(8,128)(2,1)S(1)}, bf16[392,1024]{1,0:T(8,128)(2,1)}, u32[]{:S(2)}, u32[]{:S(2)}) collective-permute-start(bf16[392,1024]{1,0:T(8,128)(2,1)S(1)} %pack.1.own_ref), channel_id=1, source_target_pairs={{0,1},{1,0},{2,3},{3,2},{4,5},{5,4},{6,7},{7,6},{8,9},{9,8},{10,11... | collective-permute-start | bytes 2408456 | tf_op jit(solution)/shard_map/ppermute | solution.py:47
  22.5 23.4 %collective-permute-start.3 = (bf16[392,1024]{1,0:T(8,128)(2,1)S(1)}, bf16[392,1024]{1,0:T(8,128)(2,1)}, u32[]{:S(2)}, u32[]{:S(2)}) collective-permute-start(bf16[392,1024]{1,0:T(8,128)(2,1)S(1)} %pack.1.own_ref), channel_id=1, source_target_pairs={{1,2},{2,1},{3,0},{0,3},{5,6},{6,5},{7,4},{4,7},{9,10},{10,9},{11,... | collective-permute-start | bytes 2408456 | tf_op jit(solution)/shard_map/ppermute | solution.py:47
  25.2 27.6 %collective-permute-start.5 = (bf16[392,1024]{1,0:T(8,128)(2,1)S(1)}, bf16[392,1024]{1,0:T(8,128)(2,1)S(1)}, u32[]{:S(2)}, u32[]{:S(2)}) collective-permute-start(bf16[392,1024]{1,0:T(8,128)(2,1)S(1)} %collective-permute-done.refs_0_), channel_id=1, source_target_pairs={{0,4},{1,5},{4,8},{5,9},{8,12},{9,13},{12,16},{13,17},{16,20},{17,... | collective-permute-start | bytes 2408456 | tf_op jit(solution)/shard_map/ppermute | solution.py:47
  38.3 21.8 %collective-permute-start.6 = (bf16[392,1024]{1,0:T(8,128)(2,1)S(1)}, bf16[392,1024]{1,0:T(8,128)(2,1)S(1)}, u32[]{:S(2)}, u32[]{:S(2)}) collective-permute-start(bf16[392,1024]{1,0:T(8,128)(2,1)S(1)} %get-tuple-element.15), channel_id=1, source_target_pairs={{0,1},{1,0},{2,3},{3,2},{4,5},{5,4},{6,7},{7,6},{8,9},{9,8},{10,11... | collective-permute-start | bytes 2408456 | tf_op jit(solution)/shard_map/ppermute | solution.py:47
  40.8 22.7 %collective-permute-start.7 = (bf16[392,1024]{1,0:T(8,128)(2,1)S(1)}, bf16[392,1024]{1,0:T(8,128)(2,1)S(1)}, u32[]{:S(2)}, u32[]{:S(2)}) collective-permute-start(bf16[392,1024]{1,0:T(8,128)(2,1)S(1)} %get-tuple-element.14), channel_id=1, source_target_pairs={{1,2},{2,1},{3,0},{0,3},{5,6},{6,5},{7,4},{4,7},{9,10},{10,9},{11,... | collective-permute-start | bytes 2408456 | tf_op jit(solution)/shard_map/ppermute | solution.py:47

commit v4 on v3

--- a/solution.py
+++ b/solution.py
@@ -12,7 +12,8 @@
 ROWS = 384
 RING = 4
 CHUNKS = 2
-TAIL = 8
+LANES = 128
+TAIL = 16
 VMEM_BYTES = 40 * 1024 * 1024
 
 
@@ -23,14 +24,6 @@
             for column in columns:
                 target = (column + along) % RING
                 pairs.append((plane * RING + column, (plane + up) * RING + target))
-    return pairs
-
-
-def swaps(total, stride, start):
-    pairs = []
-    for low in range(start * stride, total - stride, 2 * stride):
-        for device in range(low, low + stride):
-            pairs += [(device, device + stride), (device + stride, device)]
     return pairs
 
 
@@ -58,20 +51,30 @@
     label_copy.start()
     for copy in copies:
         copy.start()
-    packed_ref[rows:, rows:] = jnp.zeros((TAIL, width - rows), jnp.bfloat16)
+    slabs = width // LANES
     label_copy.wait()
-    label = (label_ref[...].reshape(1, rows) + 1).astype(jnp.float32).astype(jnp.bfloat16)
-    packed_ref[rows:, :rows] = jnp.broadcast_to(label, (TAIL, rows))
-    for copy, chunk in zip(copies, chunks):
+    label = (label_ref[...].reshape(1, rows) + 1).astype(jnp.float32)
+    lines = [label[:, i : i + LANES] for i in range(0, rows, LANES)]
+    blank = jnp.zeros((TAIL - len(lines), LANES), jnp.float32)
+    packed_ref[slabs * rows :, :] = jnp.concatenate([*lines, blank], axis=0).astype(jnp.bfloat16)
+    for i, copy in enumerate(copies):
         copy.wait()
-        values = values_ref[chunk, :].astype(jnp.float32)
+        values = values_ref[chunks[i], :].astype(jnp.float32)
         scale = lax.rsqrt(jnp.mean(values * values, axis=1, keepdims=True) + 1e-06)
-        packed_ref[chunk, :] = (values * scale).astype(jnp.bfloat16)
+        unit = (values * scale).astype(jnp.bfloat16)
+        for slab in range(slabs):
+            first = slab * rows + i * (rows // CHUNKS)
+            packed_ref[first : first + rows // CHUNKS, :] = unit[:, slab * LANES : (slab + 1) * LANES]
 
 
-def labels_of(tail_ref):
-    rows = tail_ref.shape[0] - TAIL
-    return tail_ref[rows:, :ROWS].astype(jnp.float32)[:1, :]
+def rows_of(block_ref):
+    slabs = (block_ref.shape[0] - TAIL) // ROWS
+    return jnp.concatenate([block_ref[i * ROWS : (i + 1) * ROWS, :] for i in range(slabs)], axis=1)
+
+
+def labels_of(block_ref):
+    tail = block_ref[block_ref.shape[0] - TAIL :, :].astype(jnp.float32)
+    return jnp.concatenate([tail[i : i + 1] for i in range(ROWS // LANES)], axis=1)
 
 
 def tile(own, own_label, far, far_label, kernel_scale, diagonal):
@@ -90,24 +93,20 @@
     return pull, jnp.sum(weight, axis=1, keepdims=True)
 
 
-def block_kernel(kernel_scale, fresh, final, n_blocks, n_halves, own_ref, *refs):
+def block_kernel(kernel_scale, fresh, final, own_ref, *refs):
     refs, (sum_ref, count_ref) = refs[:-2], refs[-2:]
-    rows = own_ref.shape[0] - TAIL
-    own = own_ref[:rows, :]
-    own_row = labels_of(own_ref)
-    own_label = jnp.broadcast_to(own_row, (128, rows)).T[:, :1]
+    own, own_row = rows_of(own_ref), labels_of(own_ref)
+    rows = own.shape[0]
+    own_label = jnp.broadcast_to(own_row, (LANES, rows)).T[:, :1]
     if fresh:
         pulled, counted = tile(own, own_label, own, own_row, kernel_scale, True)
     else:
         pulled, counted = refs[0][...], refs[1][:, :1]
         refs = refs[2:]
-    parts = [(ref[:rows, :], labels_of(ref)) for ref in refs[:n_blocks]]
-    for i in range(n_halves):
-        top, bottom = refs[n_blocks + 2 * i], refs[n_blocks + 2 * i + 1]
-        label, half = labels_of(bottom), top.shape[0]
-        parts += [(top[...], label[:, :half]), (bottom[: rows - half, :], label[:, half:])]
-    for far, far_label in parts:
-        pull, count = tile(own, own_label, far, far_label, kernel_scale, False)
+    for far_ref in refs:
+        pull, count = tile(
+            own, own_label, rows_of(far_ref), labels_of(far_ref), kernel_scale, False
+        )
         pulled, counted = pulled + pull, counted + count
     if final:
         sum_ref[...] = pulled * (1.0 / (1.0 + counted))
@@ -131,7 +130,7 @@
     total = lax.axis_size("grp") * lax.axis_size("dev")
     kernel_scale = 2.0 / math.sqrt(width)
     params = pltpu.CompilerParams(vmem_limit_bytes=VMEM_BYTES)
-    block = jax.ShapeDtypeStruct((rows + TAIL, width), jnp.bfloat16)
+    block = jax.ShapeDtypeStruct((width // LANES * rows + TAIL, LANES), jnp.bfloat16)
     sums = jax.ShapeDtypeStruct((rows, width), jnp.float32)
     counts = jax.ShapeDtypeStruct((rows, 128), jnp.float32)
     own = pl.pallas_call(
@@ -150,16 +149,15 @@
         pltpu.with_memory_space_constraint(cluster_ids, pltpu.HBM),
     )
     column = lax.rem(lax.axis_index("dev"), RING)
-    odd = lax.rem(lax.axis_index("dev") // RING, 2)
 
-    def add(state, blocks, halves, final, name):
+    def add(state, blocks, final, name):
         return pl.pallas_call(
-            functools.partial(block_kernel, kernel_scale, not state, final, len(blocks), len(halves) // 2),
+            functools.partial(block_kernel, kernel_scale, not state, final),
             out_shape=(sums, jax.ShapeDtypeStruct((rows,), jnp.float32) if final else counts),
             compiler_params=params,
-            cost_estimate=cost(len(blocks) + len(halves) // 2 + (not state), rows, width),
+            cost_estimate=cost(len(blocks) + (not state), rows, width),
             name=name,
-        )(own, *state, *blocks, *halves)
+        )(own, *state, *blocks)
 
     across = send(own, plane_pairs(total, 0, 2))
     below = send(own, plane_pairs(total, 1, 0))
@@ -172,10 +170,10 @@
     corner = send(across, climb)
     first_side = send(jnp.where(lax.rem(column, 2) == 1, below, above), ring_swaps(total, 0))
     second_side = send(jnp.where(column >= RING // 2, below, above), ring_swaps(total, 1))
-    state = add((), (across, above, below, second_column, first_column), (), False, "near")
-    state = add(state, (corner,), (), False, "corner")
-    state = add(state, (first_side,), (), False, "side")
-    return add(state, (second_side,), (), True, "late")
+    state = add((), (across, above, below, second_column, first_column), False, "near")
+    state = add(state, (corner,), False, "corner")
+    state = add(state, (first_side,), False, "side")
+    return add(state, (second_side,), True, "late")
 
 
 def solution(mesh):

time: 66.2 us -> 65.7 us (level)
  transfers between devices with their start and end apart: 8 -> 8, of which waited for: 6 -> 5; matrix products, arithmetic and copies ran while one was open for 0% -> 0% of each run, Pallas kernels for 14% -> 14%
where the time goes in v4:
time: 65.7 us; the launch traced here: 65.4 us
  starting transfers between devices  32.6 us (50%)
  waiting for transfers between devices  19.3 us (29%)
  Pallas kernels  12.6 us (19%)
  between operations  0.77 us (1%)
    ppermute x8, starting transfers between devices, send(): return lax.ppermute(block, AXES, pairs)  32.6 us
    ppermute x8, waiting for transfers between devices, send(): return lax.ppermute(block, AXES, pairs)  19.3 us
    pallas_call x4, Pallas kernels, add(): pl.pallas_call(functools.partial(block_kernel, kernel_scale, not state, f...  11.3 us
    pallas_call x1, Pallas kernels, shards(): pl.pallas_call(pack_kernel, out_shape=block, in_specs=[pl.BlockSpec(memor...  1.38 us
  transfers between devices with their start and end apart: 8, of which 5 were waited for; matrix products, arithmetic and copies ran while one was open for 0% of the time, Pallas kernels for 14%

profile of v4, /device:TPU:6, one launch (start us, length us, event | category | flops | bytes accessed | tf_op | source)
XLA Modules:
  0.0 65.4 jit_solution(10234518598964970256)
XLA Ops:
  0.6 1.4 %pack.1.own_ref = bf16[3088,128]{1,0:T(8,128)(2,1)S(1)} custom-call(bf16[384,1024]{1,0:T(8,128)(2,1)} %values_hbm.1, s32[384]{0:T(512)} %label_hbm.1), custom_call_target="tpu_custom_call" | custom-call | tf_op jit(solution)/shard_map/pack/pallas_call | solution.py:136
  2.0 5.1 %collective-permute-start = (bf16[3088,128]{1,0:T(8,128)(2,1)S(1)}, bf16[3088,128]{1,0:T(8,128)(2,1)S(1)}, u32[]{:S(2)}, u32[]{:S(2)}) collective-permute-start(bf16[3088,128]{1,0:T(8,128)(2,1)S(1)} %pack.1.own_ref), channel_id=1, source_target_pairs={{0,2},{1,3},{2,0},{3,1},{4,6},{5,7},{6,4},{7,5},{8,10},{9,11},{10,... | collective-permute-start | bytes 2371592 | tf_op jit(solution)/shard_map/ppermute | solution.py:40
  7.1 3.8 %collective-permute-start.2 = (bf16[3088,128]{1,0:T(8,128)(2,1)S(1)}, bf16[3088,128]{1,0:T(8,128)(2,1)S(1)}, u32[]{:S(2)}, u32[]{:S(2)}) collective-permute-start(bf16[3088,128]{1,0:T(8,128)(2,1)S(1)} %pack.1.own_ref), channel_id=1, source_target_pairs={{0,4},{1,5},{2,6},{3,7},{4,8},{5,9},{6,10},{7,11},{8,12},{9,13},{1... | collective-permute-start | bytes 2371592 | tf_op jit(solution)/shard_map/ppermute | solution.py:40
  11.0 8.9 %collective-permute-start.1 = (bf16[3088,128]{1,0:T(8,128)(2,1)S(1)}, bf16[3088,128]{1,0:T(8,128)(2,1)S(1)}, u32[]{:S(2)}, u32[]{:S(2)}) collective-permute-start(bf16[3088,128]{1,0:T(8,128)(2,1)S(1)} %pack.1.own_ref), channel_id=1, source_target_pairs={{4,0},{5,1},{6,2},{7,3},{8,4},{9,5},{10,6},{11,7},{12,8},{13,9},{1... | collective-permute-start | bytes 2371592 | tf_op jit(solution)/shard_map/ppermute | solution.py:40
  19.9 2.6 %collective-permute-start.4 = (bf16[3088,128]{1,0:T(8,128)(2,1)S(1)}, bf16[3088,128]{1,0:T(8,128)(2,1)}, u32[]{:S(2)}, u32[]{:S(2)}) collective-permute-start(bf16[3088,128]{1,0:T(8,128)(2,1)S(1)} %pack.1.own_ref), channel_id=1, source_target_pairs={{0,1},{1,0},{2,3},{3,2},{4,5},{5,4},{6,7},{7,6},{8,9},{9,8},{10,11... | collective-permute-start | bytes 2371592 | tf_op jit(solution)/shard_map/ppermute | solution.py:40
  22.5 2.3 %collective-permute-start.3 = (bf16[3088,128]{1,0:T(8,128)(2,1)S(1)}, bf16[3088,128]{1,0:T(8,128)(2,1)}, u32[]{:S(2)}, u32[]{:S(2)}) collective-permute-start(bf16[3088,128]{1,0:T(8,128)(2,1)S(1)} %pack.1.own_ref), channel_id=1, source_target_pairs={{1,2},{2,1},{3,0},{0,3},{5,6},{6,5},{7,4},{4,7},{9,10},{10,9},{11,... | collective-permute-start | bytes 2371592 | tf_op jit(solution)/shard_map/ppermute | solution.py:40
  24.8 0.0 collective-permute-done.refs_0_
  24.8 5.0 %collective-permute-start.5 = (bf16[3088,128]{1,0:T(8,128)(2,1)S(1)}, bf16[3088,128]{1,0:T(8,128)(2,1)S(1)}, u32[]{:S(2)}, u32[]{:S(2)}) collective-permute-start(bf16[3088,128]{1,0:T(8,128)(2,1)S(1)} %collective-permute-done.refs_0_), channel_id=1, source_target_pairs={{0,4},{1,5},{4,8},{5,9},{8,12},{9,13},{12,16},{13,17},{16,20},{17,... | collective-permute-start | bytes 2371592 | tf_op jit(solution)/shard_map/ppermute | solution.py:40
  29.8 5.2 %collective-permute-done.2.refs_2_ = bf16[3088,128]{1,0:T(8,128)(2,1)S(1)} collective-permute-done((bf16[3088,128]{1,0:T(8,128)(2,1)S(1)}, bf16[3088,128]{1,0:T(8,128)(2,1)S(1)}, u32[]{:S(2)}, u32[]{:S(2)}) %collective-permute-start.2) | collective-permute-done | bytes 790560 | tf_op jit(solution)/shard_map/ppermute | solution.py:40
  35.0 2.9 %collective-permute-done.1.refs_1_ = bf16[3088,128]{1,0:T(8,128)(2,1)S(1)} collective-permute-done((bf16[3088,128]{1,0:T(8,128)(2,1)S(1)}, bf16[3088,128]{1,0:T(8,128)(2,1)S(1)}, u32[]{:S(2)}, u32[]{:S(2)}) %collective-permute-start.1) | collective-permute-done | bytes 790560 | tf_op jit(solution)/shard_map/ppermute | solution.py:40
  37.9 0.1 broadcast_select_fusion
  38.0 2.6 %collective-permute-start.6 = (bf16[3088,128]{1,0:T(8,128)(2,1)S(1)}, bf16[3088,128]{1,0:T(8,128)(2,1)S(1)}, u32[]{:S(2)}, u32[]{:S(2)}) collective-permute-start(bf16[3088,128]{1,0:T(8,128)(2,1)S(1)} %get-tuple-element.15), channel_id=1, source_target_pairs={{0,1},{1,0},{2,3},{3,2},{4,5},{5,4},{6,7},{7,6},{8,9},{9,8},{10,11... | collective-permute-start | bytes 2371592 | tf_op jit(solution)/shard_map/ppermute | solution.py:40
  40.6 2.3 %collective-permute-start.7 = (bf16[3088,128]{1,0:T(8,128)(2,1)S(1)}, bf16[3088,128]{1,0:T(8,128)(2,1)S(1)}, u32[]{:S(2)}, u32[]{:S(2)}) collective-permute-start(bf16[3088,128]{1,0:T(8,128)(2,1)S(1)} %get-tuple-element.14), channel_id=1, source_target_pairs={{1,2},{2,1},{3,0},{0,3},{5,6},{6,5},{7,4},{4,7},{9,10},{10,9},{11,... | collective-permute-start | bytes 2371592 | tf_op jit(solution)/shard_map/ppermute | solution.py:40
  42.9 0.0 collective-permute-done.4.refs_4_
  42.9 2.7 %collective-permute-done.3.refs_3_ = bf16[3088,128]{1,0:T(8,128)(2,1)} collective-permute-done((bf16[3088,128]{1,0:T(8,128)(2,1)S(1)}, bf16[3088,128]{1,0:T(8,128)(2,1)}, u32[]{:S(2)}, u32[]{:S(2)}) %collective-permute-start.3) | collective-permute-done | bytes 790560 | tf_op jit(solution)/shard_map/ppermute | solution.py:40
  45.7 6.8 %near.1 = (f32[384,1024]{1,0:T(8,128)S(1)}, f32[384,128]{1,0:T(8,128)S(1)}) custom-call(bf16[3088,128]{1,0:T(8,128)(2,1)S(1)} %pack.1.own_ref, bf16[3088,128]{1,0:T(8,128)(2,1)S(1)} %collective-permute-done.refs_0_, bf16[3088,128]{1,0:T(8,128)(2,1)S(1)} %collective-permute-done.1.refs_1_, bf16[3088,128]{1,0:T(8,128)(2,1)S(1)} %collective-permute-done.2.refs_2_, ...), custom_call_target="tpu_custom_call" | custom-call | flops 3623878656 | bytes 5505024 | tf_op jit(solution)/shard_map/near/pallas_call | solution.py:154
  52.5 0.0 collective-permute-done.5.refs_2_
  52.5 1.1 %corner.1 = (f32[384,1024]{1,0:T(8,128)S(1)}, f32[384,128]{1,0:T(8,128)S(1)}) custom-call(bf16[3088,128]{1,0:T(8,128)(2,1)S(1)} %pack.1.own_ref, f32[384,1024]{1,0:T(8,128)S(1)} %get-tuple-element.8.refs_0_, f32[384,128]{1,0:T(8,128)S(1)} %get-tuple-element.9.refs_1_, bf16[3088,128]{1,0:T(8,128)(2,1)S(1)} %collective-permute-done.5.refs_2_), custom_call_target="tpu_custom_call" | custom-call | flops 603979776 | bytes 1572864 | tf_op jit(solution)/shard_map/corner/pallas_call | solution.py:154
  53.6 6.0 %collective-permute-done.6.refs_2_ = bf16[3088,128]{1,0:T(8,128)(2,1)S(1)} collective-permute-done((bf16[3088,128]{1,0:T(8,128)(2,1)S(1)}, bf16[3088,128]{1,0:T(8,128)(2,1)S(1)}, u32[]{:S(2)}, u32[]{:S(2)}) %collective-permute-start.6) | collective-permute-done | bytes 790560 | tf_op jit(solution)/shard_map/ppermute | solution.py:40
  59.5 1.1 %side.1 = (f32[384,1024]{1,0:T(8,128)S(1)}, f32[384,128]{1,0:T(8,128)S(1)}) custom-call(bf16[3088,128]{1,0:T(8,128)(2,1)S(1)} %pack.1.own_ref, f32[384,1024]{1,0:T(8,128)S(1)} %get-tuple-element.10.refs_0_, f32[384,128]{1,0:T(8,128)S(1)} %get-tuple-element.11.refs_1_, bf16[3088,128]{1,0:T(8,128)(2,1)S(1)} %collective-permute-done.6.refs_2_), custom_call_target="tpu_custom_call" | custom-call | flops 603979776 | bytes 1572864 | tf_op jit(solution)/shard_map/side/pallas_call | solution.py:154
  60.6 2.4 %collective-permute-done.7.refs_2_ = bf16[3088,128]{1,0:T(8,128)(2,1)S(1)} collective-permute-done((bf16[3088,128]{1,0:T(8,128)(2,1)S(1)}, bf16[3088,128]{1,0:T(8,128)(2,1)S(1)}, u32[]{:S(2)}, u32[]{:S(2)}) %collective-permute-start.7) | collective-permute-done | bytes 790560 | tf_op jit(solution)/shard_map/ppermute | solution.py:40
  63.1 2.3 %late.1 = (f32[384,1024]{1,0:T(8,128)}, f32[384]{0:T(512)}) custom-call(bf16[3088,128]{1,0:T(8,128)(2,1)S(1)} %pack.1.own_ref, f32[384,1024]{1,0:T(8,128)S(1)} %get-tuple-element.12.refs_0_, f32[384,128]{1,0:T(8,128)S(1)} %get-tuple-element.13.refs_1_, bf16[3088,128]{1,0:T(8,128)(2,1)S(1)} %collective-permute-done.7.refs_2_), custom_call_target="tpu_custom_call" | custom-call | flops 603979776 | bytes 1572864 | tf_op jit(solution)/shard_map/late/pallas_call | solution.py:154
Async XLA Ops:
  2.0 22.8 %collective-permute-start = (bf16[3088,128]{1,0:T(8,128)(2,1)S(1)}, bf16[3088,128]{1,0:T(8,128)(2,1)S(1)}, u32[]{:S(2)}, u32[]{:S(2)}) collective-permute-start(bf16[3088,128]{1,0:T(8,128)(2,1)S(1)} %pack.1.own_ref), channel_id=1, source_target_pairs={{0,2},{1,3},{2,0},{3,1},{4,6},{5,7},{6,4},{7,5},{8,10},{9,11},{10,... | collective-permute-start | bytes 2371592 | tf_op jit(solution)/shard_map/ppermute | solution.py:40
  7.1 27.9 %collective-permute-start.2 = (bf16[3088,128]{1,0:T(8,128)(2,1)S(1)}, bf16[3088,128]{1,0:T(8,128)(2,1)S(1)}, u32[]{:S(2)}, u32[]{:S(2)}) collective-permute-start(bf16[3088,128]{1,0:T(8,128)(2,1)S(1)} %pack.1.own_ref), channel_id=1, source_target_pairs={{0,4},{1,5},{2,6},{3,7},{4,8},{5,9},{6,10},{7,11},{8,12},{9,13},{1... | collective-permute-start | bytes 2371592 | tf_op jit(solution)/shard_map/ppermute | solution.py:40
  11.0 26.9 %collective-permute-start.1 = (bf16[3088,128]{1,0:T(8,128)(2,1)S(1)}, bf16[3088,128]{1,0:T(8,128)(2,1)S(1)}, u32[]{:S(2)}, u32[]{:S(2)}) collective-permute-start(bf16[3088,128]{1,0:T(8,128)(2,1)S(1)} %pack.1.own_ref), channel_id=1, source_target_pairs={{4,0},{5,1},{6,2},{7,3},{8,4},{9,5},{10,6},{11,7},{12,8},{13,9},{1... | collective-permute-start | bytes 2371592 | tf_op jit(solution)/shard_map/ppermute | solution.py:40
  19.9 23.0 %collective-permute-start.4 = (bf16[3088,128]{1,0:T(8,128)(2,1)S(1)}, bf16[3088,128]{1,0:T(8,128)(2,1)}, u32[]{:S(2)}, u32[]{:S(2)}) collective-permute-start(bf16[3088,128]{1,0:T(8,128)(2,1)S(1)} %pack.1.own_ref), channel_id=1, source_target_pairs={{0,1},{1,0},{2,3},{3,2},{4,5},{5,4},{6,7},{7,6},{8,9},{9,8},{10,11... | collective-permute-start | bytes 2371592 | tf_op jit(solution)/shard_map/ppermute | solution.py:40
  22.5 23.2 %collective-permute-start.3 = (bf16[3088,128]{1,0:T(8,128)(2,1)S(1)}, bf16[3088,128]{1,0:T(8,128)(2,1)}, u32[]{:S(2)}, u32[]{:S(2)}) collective-permute-start(bf16[3088,128]{1,0:T(8,128)(2,1)S(1)} %pack.1.own_ref), channel_id=1, source_target_pairs={{1,2},{2,1},{3,0},{0,3},{5,6},{6,5},{7,4},{4,7},{9,10},{10,9},{11,... | collective-permute-start | bytes 2371592 | tf_op jit(solution)/shard_map/ppermute | solution.py:40
  24.8 27.6 %collective-permute-start.5 = (bf16[3088,128]{1,0:T(8,128)(2,1)S(1)}, bf16[3088,128]{1,0:T(8,128)(2,1)S(1)}, u32[]{:S(2)}, u32[]{:S(2)}) collective-permute-start(bf16[3088,128]{1,0:T(8,128)(2,1)S(1)} %collective-permute-done.refs_0_), channel_id=1, source_target_pairs={{0,4},{1,5},{4,8},{5,9},{8,12},{9,13},{12,16},{13,17},{16,20},{17,... | collective-permute-start | bytes 2371592 | tf_op jit(solution)/shard_map/ppermute | solution.py:40
  38.0 21.5 %collective-permute-start.6 = (bf16[3088,128]{1,0:T(8,128)(2,1)S(1)}, bf16[3088,128]{1,0:T(8,128)(2,1)S(1)}, u32[]{:S(2)}, u32[]{:S(2)}) collective-permute-start(bf16[3088,128]{1,0:T(8,128)(2,1)S(1)} %get-tuple-element.15), channel_id=1, source_target_pairs={{0,1},{1,0},{2,3},{3,2},{4,5},{5,4},{6,7},{7,6},{8,9},{9,8},{10,11... | collective-permute-start | bytes 2371592 | tf_op jit(solution)/shard_map/ppermute | solution.py:40
  40.6 22.5 %collective-permute-start.7 = (bf16[3088,128]{1,0:T(8,128)(2,1)S(1)}, bf16[3088,128]{1,0:T(8,128)(2,1)S(1)}, u32[]{:S(2)}, u32[]{:S(2)}) collective-permute-start(bf16[3088,128]{1,0:T(8,128)(2,1)S(1)} %get-tuple-element.14), channel_id=1, source_target_pairs={{1,2},{2,1},{3,0},{0,3},{5,6},{6,5},{7,4},{4,7},{9,10},{10,9},{11,... | collective-permute-start | bytes 2371592 | tf_op jit(solution)/shard_map/ppermute | solution.py:40

commit v5 on v4

--- a/solution.py
+++ b/solution.py
@@ -12,6 +12,7 @@
 ROWS = 384
 RING = 4
 CHUNKS = 2
+PARTS = 2
 LANES = 128
 TAIL = 16
 VMEM_BYTES = 40 * 1024 * 1024
@@ -77,7 +78,11 @@
     return jnp.concatenate([tail[i : i + 1] for i in range(ROWS // LANES)], axis=1)
 
 
-def tile(own, own_label, far, far_label, kernel_scale, diagonal):
+def own_column(own_row):
+    return jnp.broadcast_to(own_row, (LANES, own_row.shape[1])).T[:, :1]
+
+
+def weights(own, own_label, far, far_label, kernel_scale, diagonal):
     scores = (
         lax.dot_general(own, far, (((1,), (1,)), ((), ())), preferred_element_type=jnp.float32)
         * kernel_scale
@@ -88,16 +93,19 @@
         linked = linked & (
             lax.broadcasted_iota(jnp.int32, shape, 0) != lax.broadcasted_iota(jnp.int32, shape, 1)
         )
-    weight = jnp.where(linked, jnp.exp(scores), 0.0)
+    return jnp.where(linked, jnp.exp(scores), 0.0)
+
+
+def tile(own, own_label, far, far_label, kernel_scale, diagonal):
+    weight = weights(own, own_label, far, far_label, kernel_scale, diagonal)
     pull = jnp.dot(weight.astype(jnp.bfloat16), far, preferred_element_type=jnp.float32)
     return pull, jnp.sum(weight, axis=1, keepdims=True)
 
 
-def block_kernel(kernel_scale, fresh, final, own_ref, *refs):
+def block_kernel(kernel_scale, fresh, own_ref, *refs):
     refs, (sum_ref, count_ref) = refs[:-2], refs[-2:]
     own, own_row = rows_of(own_ref), labels_of(own_ref)
-    rows = own.shape[0]
-    own_label = jnp.broadcast_to(own_row, (LANES, rows)).T[:, :1]
+    own_label = own_column(own_row)
     if fresh:
         pulled, counted = tile(own, own_label, own, own_row, kernel_scale, True)
     else:
@@ -108,13 +116,45 @@
             own, own_label, rows_of(far_ref), labels_of(far_ref), kernel_scale, False
         )
         pulled, counted = pulled + pull, counted + count
-    if final:
-        sum_ref[...] = pulled * (1.0 / (1.0 + counted))
-        logs = jnp.log(1.0 + jnp.broadcast_to(counted, (rows, 128)).T[:1, :])
-        count_ref[...] = logs.reshape(rows)
-    else:
-        sum_ref[...] = pulled
-        count_ref[...] = jnp.broadcast_to(counted, count_ref.shape)
+    sum_ref[...] = pulled
+    count_ref[...] = jnp.broadcast_to(counted, count_ref.shape)
+
+
+def last_kernel(
+    kernel_scale,
+    own_ref,
+    sum_ref,
+    count_ref,
+    far_ref,
+    mean_hbm,
+    log_hbm,
+    mean_ref,
+    log_ref,
+    semaphores,
+):
+    own, far = rows_of(own_ref), rows_of(far_ref)
+    own_label = own_column(labels_of(own_ref))
+    weight = weights(own, own_label, far, labels_of(far_ref), kernel_scale, False)
+    counted = count_ref[:, :1] + jnp.sum(weight, axis=1, keepdims=True)
+    share = 1.0 / (1.0 + counted)
+    rounded = weight.astype(jnp.bfloat16)
+    rows = own.shape[0]
+    step, copies = rows // PARTS, []
+    for part in range(PARTS):
+        first, end = part * step, (part + 1) * step
+        pull = jnp.dot(rounded[first:end], far, preferred_element_type=jnp.float32)
+        mean_ref[first:end, :] = (sum_ref[first:end, :] + pull) * share[first:end]
+        chunk = pl.ds(first, step)
+        copies.append(
+            pltpu.make_async_copy(mean_ref.at[chunk], mean_hbm.at[chunk], semaphores.at[part])
+        )
+        copies[-1].start()
+    logs = jnp.log(1.0 + jnp.broadcast_to(counted, (rows, LANES)).T[:1, :])
+    log_ref[...] = logs.reshape(rows)
+    copies.append(pltpu.make_async_copy(log_ref, log_hbm, semaphores.at[PARTS]))
+    copies[-1].start()
+    for copy in copies:
+        copy.wait()
 
 
 def cost(tiles, rows, width):
@@ -150,10 +190,10 @@
     )
     column = lax.rem(lax.axis_index("dev"), RING)
 
-    def add(state, blocks, final, name):
+    def add(state, blocks, name):
         return pl.pallas_call(
-            functools.partial(block_kernel, kernel_scale, not state, final),
-            out_shape=(sums, jax.ShapeDtypeStruct((rows,), jnp.float32) if final else counts),
+            functools.partial(block_kernel, kernel_scale, not state),
+            out_shape=(sums, counts),
             compiler_params=params,
             cost_estimate=cost(len(blocks) + (not state), rows, width),
             name=name,
@@ -170,10 +210,22 @@
     corner = send(across, climb)
     first_side = send(jnp.where(lax.rem(column, 2) == 1, below, above), ring_swaps(total, 0))
     second_side = send(jnp.where(column >= RING // 2, below, above), ring_swaps(total, 1))
-    state = add((), (across, above, below, second_column, first_column), False, "near")
-    state = add(state, (corner,), False, "corner")
-    state = add(state, (first_side,), False, "side")
-    return add(state, (second_side,), True, "late")
+    state = add((), (across, above, below, second_column, first_column), "near")
+    state = add(state, (corner,), "corner")
+    state = add(state, (first_side,), "side")
+    return pl.pallas_call(
+        functools.partial(last_kernel, kernel_scale),
+        out_shape=(sums, jax.ShapeDtypeStruct((rows,), jnp.float32)),
+        out_specs=(pl.BlockSpec(memory_space=pl.ANY),) * 2,
+        scratch_shapes=[
+            pltpu.VMEM((rows, width), jnp.float32),
+            pltpu.VMEM((rows,), jnp.float32),
+            pltpu.SemaphoreType.DMA((PARTS + 1,)),
+        ],
+        compiler_params=params,
+        cost_estimate=cost(1, rows, width),
+        name="late",
+    )(own, *state, second_side)
 
 
 def solution(mesh):

time: 65.7 us -> 65.5 us (level)
  no operation moved by 1% of the time
where the time goes in v5:
time: 65.5 us; the launch traced here: 65.2 us
  starting transfers between devices  32.6 us (50%)
  waiting for transfers between devices  19.3 us (29%)
  Pallas kernels  12.5 us (19%)
  between operations  0.77 us (1%)
    ppermute x8, starting transfers between devices, send(): return lax.ppermute(block, AXES, pairs)  32.6 us
    ppermute x8, waiting for transfers between devices, send(): return lax.ppermute(block, AXES, pairs)  19.3 us
    pallas_call x3, Pallas kernels, add(): pl.pallas_call(functools.partial(block_kernel, kernel_scale, not state),...  8.97 us
    pallas_call x1, Pallas kernels, shards(): pl.pallas_call(functools.partial(last_kernel, kernel_scale), out_shape=(s...  2.13 us
    pallas_call x1, Pallas kernels, shards(): pl.pallas_call(pack_kernel, out_shape=block, in_specs=[pl.BlockSpec(memor...  1.38 us
  transfers between devices with their start and end apart: 8, of which 5 were waited for; matrix products, arithmetic and copies ran while one was open for 0% of the time, Pallas kernels for 14%

profile of v5, /device:TPU:6, one launch (start us, length us, event | category | flops | bytes accessed | tf_op | source)
XLA Modules:
  0.0 65.2 jit_solution(5794204433718469521)
XLA Ops:
  0.6 1.4 %pack.1.own_ref = bf16[3088,128]{1,0:T(8,128)(2,1)S(1)} custom-call(bf16[384,1024]{1,0:T(8,128)(2,1)} %values_hbm.1, s32[384]{0:T(512)} %label_hbm.1), custom_call_target="tpu_custom_call" | custom-call | tf_op jit(solution)/shard_map/pack/pallas_call | solution.py:176
  2.0 5.1 %collective-permute-start = (bf16[3088,128]{1,0:T(8,128)(2,1)S(1)}, bf16[3088,128]{1,0:T(8,128)(2,1)S(1)}, u32[]{:S(2)}, u32[]{:S(2)}) collective-permute-start(bf16[3088,128]{1,0:T(8,128)(2,1)S(1)} %pack.1.own_ref), channel_id=1, source_target_pairs={{0,2},{1,3},{2,0},{3,1},{4,6},{5,7},{6,4},{7,5},{8,10},{9,11},{10,... | collective-permute-start | bytes 2371592 | tf_op jit(solution)/shard_map/ppermute | solution.py:41
  7.1 3.8 %collective-permute-start.2 = (bf16[3088,128]{1,0:T(8,128)(2,1)S(1)}, bf16[3088,128]{1,0:T(8,128)(2,1)S(1)}, u32[]{:S(2)}, u32[]{:S(2)}) collective-permute-start(bf16[3088,128]{1,0:T(8,128)(2,1)S(1)} %pack.1.own_ref), channel_id=1, source_target_pairs={{0,4},{1,5},{2,6},{3,7},{4,8},{5,9},{6,10},{7,11},{8,12},{9,13},{1... | collective-permute-start | bytes 2371592 | tf_op jit(solution)/shard_map/ppermute | solution.py:41
  11.0 8.9 %collective-permute-start.1 = (bf16[3088,128]{1,0:T(8,128)(2,1)S(1)}, bf16[3088,128]{1,0:T(8,128)(2,1)S(1)}, u32[]{:S(2)}, u32[]{:S(2)}) collective-permute-start(bf16[3088,128]{1,0:T(8,128)(2,1)S(1)} %pack.1.own_ref), channel_id=1, source_target_pairs={{4,0},{5,1},{6,2},{7,3},{8,4},{9,5},{10,6},{11,7},{12,8},{13,9},{1... | collective-permute-start | bytes 2371592 | tf_op jit(solution)/shard_map/ppermute | solution.py:41
  19.9 2.6 %collective-permute-start.4 = (bf16[3088,128]{1,0:T(8,128)(2,1)S(1)}, bf16[3088,128]{1,0:T(8,128)(2,1)}, u32[]{:S(2)}, u32[]{:S(2)}) collective-permute-start(bf16[3088,128]{1,0:T(8,128)(2,1)S(1)} %pack.1.own_ref), channel_id=1, source_target_pairs={{0,1},{1,0},{2,3},{3,2},{4,5},{5,4},{6,7},{7,6},{8,9},{9,8},{10,11... | collective-permute-start | bytes 2371592 | tf_op jit(solution)/shard_map/ppermute | solution.py:41
  22.5 2.3 %collective-permute-start.3 = (bf16[3088,128]{1,0:T(8,128)(2,1)S(1)}, bf16[3088,128]{1,0:T(8,128)(2,1)}, u32[]{:S(2)}, u32[]{:S(2)}) collective-permute-start(bf16[3088,128]{1,0:T(8,128)(2,1)S(1)} %pack.1.own_ref), channel_id=1, source_target_pairs={{1,2},{2,1},{3,0},{0,3},{5,6},{6,5},{7,4},{4,7},{9,10},{10,9},{11,... | collective-permute-start | bytes 2371592 | tf_op jit(solution)/shard_map/ppermute | solution.py:41
  24.8 0.0 collective-permute-done.refs_0_
  24.8 5.0 %collective-permute-start.5 = (bf16[3088,128]{1,0:T(8,128)(2,1)S(1)}, bf16[3088,128]{1,0:T(8,128)(2,1)S(1)}, u32[]{:S(2)}, u32[]{:S(2)}) collective-permute-start(bf16[3088,128]{1,0:T(8,128)(2,1)S(1)} %collective-permute-done.refs_0_), channel_id=1, source_target_pairs={{0,4},{1,5},{4,8},{5,9},{8,12},{9,13},{12,16},{13,17},{16,20},{17,... | collective-permute-start | bytes 2371592 | tf_op jit(solution)/shard_map/ppermute | solution.py:41
  29.8 5.2 %collective-permute-done.2.refs_2_ = bf16[3088,128]{1,0:T(8,128)(2,1)S(1)} collective-permute-done((bf16[3088,128]{1,0:T(8,128)(2,1)S(1)}, bf16[3088,128]{1,0:T(8,128)(2,1)S(1)}, u32[]{:S(2)}, u32[]{:S(2)}) %collective-permute-start.2) | collective-permute-done | bytes 790560 | tf_op jit(solution)/shard_map/ppermute | solution.py:41
  35.0 2.9 %collective-permute-done.1.refs_1_ = bf16[3088,128]{1,0:T(8,128)(2,1)S(1)} collective-permute-done((bf16[3088,128]{1,0:T(8,128)(2,1)S(1)}, bf16[3088,128]{1,0:T(8,128)(2,1)S(1)}, u32[]{:S(2)}, u32[]{:S(2)}) %collective-permute-start.1) | collective-permute-done | bytes 790560 | tf_op jit(solution)/shard_map/ppermute | solution.py:41
  37.9 0.1 broadcast_select_fusion
  38.0 2.6 %collective-permute-start.6 = (bf16[3088,128]{1,0:T(8,128)(2,1)S(1)}, bf16[3088,128]{1,0:T(8,128)(2,1)S(1)}, u32[]{:S(2)}, u32[]{:S(2)}) collective-permute-start(bf16[3088,128]{1,0:T(8,128)(2,1)S(1)} %get-tuple-element.15), channel_id=1, source_target_pairs={{0,1},{1,0},{2,3},{3,2},{4,5},{5,4},{6,7},{7,6},{8,9},{9,8},{10,11... | collective-permute-start | bytes 2371592 | tf_op jit(solution)/shard_map/ppermute | solution.py:41
  40.6 2.3 %collective-permute-start.7 = (bf16[3088,128]{1,0:T(8,128)(2,1)S(1)}, bf16[3088,128]{1,0:T(8,128)(2,1)S(1)}, u32[]{:S(2)}, u32[]{:S(2)}) collective-permute-start(bf16[3088,128]{1,0:T(8,128)(2,1)S(1)} %get-tuple-element.14), channel_id=1, source_target_pairs={{1,2},{2,1},{3,0},{0,3},{5,6},{6,5},{7,4},{4,7},{9,10},{10,9},{11,... | collective-permute-start | bytes 2371592 | tf_op jit(solution)/shard_map/ppermute | solution.py:41
  42.9 0.0 collective-permute-done.4.refs_4_
  42.9 2.7 %collective-permute-done.3.refs_3_ = bf16[3088,128]{1,0:T(8,128)(2,1)} collective-permute-done((bf16[3088,128]{1,0:T(8,128)(2,1)S(1)}, bf16[3088,128]{1,0:T(8,128)(2,1)}, u32[]{:S(2)}, u32[]{:S(2)}) %collective-permute-start.3) | collective-permute-done | bytes 790560 | tf_op jit(solution)/shard_map/ppermute | solution.py:41
  45.7 6.8 %near.1 = (f32[384,1024]{1,0:T(8,128)S(1)}, f32[384,128]{1,0:T(8,128)S(1)}) custom-call(bf16[3088,128]{1,0:T(8,128)(2,1)S(1)} %pack.1.own_ref, bf16[3088,128]{1,0:T(8,128)(2,1)S(1)} %collective-permute-done.refs_0_, bf16[3088,128]{1,0:T(8,128)(2,1)S(1)} %collective-permute-done.1.refs_1_, bf16[3088,128]{1,0:T(8,128)(2,1)S(1)} %collective-permute-done.2.refs_2_, ...), custom_call_target="tpu_custom_call" | custom-call | flops 3623878656 | bytes 5505024 | tf_op jit(solution)/shard_map/near/pallas_call | solution.py:194
  52.5 0.0 collective-permute-done.5.refs_2_
  52.5 1.1 %corner.1 = (f32[384,1024]{1,0:T(8,128)S(1)}, f32[384,128]{1,0:T(8,128)S(1)}) custom-call(bf16[3088,128]{1,0:T(8,128)(2,1)S(1)} %pack.1.own_ref, f32[384,1024]{1,0:T(8,128)S(1)} %get-tuple-element.8.refs_0_, f32[384,128]{1,0:T(8,128)S(1)} %get-tuple-element.9.refs_1_, bf16[3088,128]{1,0:T(8,128)(2,1)S(1)} %collective-permute-done.5.refs_2_), custom_call_target="tpu_custom_call" | custom-call | flops 603979776 | bytes 1572864 | tf_op jit(solution)/shard_map/corner/pallas_call | solution.py:194
  53.6 6.0 %collective-permute-done.6.refs_2_ = bf16[3088,128]{1,0:T(8,128)(2,1)S(1)} collective-permute-done((bf16[3088,128]{1,0:T(8,128)(2,1)S(1)}, bf16[3088,128]{1,0:T(8,128)(2,1)S(1)}, u32[]{:S(2)}, u32[]{:S(2)}) %collective-permute-start.6) | collective-permute-done | bytes 790560 | tf_op jit(solution)/shard_map/ppermute | solution.py:41
  59.5 1.1 %side.1 = (f32[384,1024]{1,0:T(8,128)S(1)}, f32[384,128]{1,0:T(8,128)S(1)}) custom-call(bf16[3088,128]{1,0:T(8,128)(2,1)S(1)} %pack.1.own_ref, f32[384,1024]{1,0:T(8,128)S(1)} %get-tuple-element.10.refs_0_, f32[384,128]{1,0:T(8,128)S(1)} %get-tuple-element.11.refs_1_, bf16[3088,128]{1,0:T(8,128)(2,1)S(1)} %collective-permute-done.6.refs_2_), custom_call_target="tpu_custom_call" | custom-call | flops 603979776 | bytes 1572864 | tf_op jit(solution)/shard_map/side/pallas_call | solution.py:194
  60.6 2.4 %collective-permute-done.7.far_ref = bf16[3088,128]{1,0:T(8,128)(2,1)S(1)} collective-permute-done((bf16[3088,128]{1,0:T(8,128)(2,1)S(1)}, bf16[3088,128]{1,0:T(8,128)(2,1)S(1)}, u32[]{:S(2)}, u32[]{:S(2)}) %collective-permute-start.7) | collective-permute-done | bytes 790560 | tf_op jit(solution)/shard_map/ppermute | solution.py:41
  63.1 2.1 %late.1 = (f32[384,1024]{1,0:T(8,128)}, f32[384]{0:T(512)}) custom-call(bf16[3088,128]{1,0:T(8,128)(2,1)S(1)} %pack.1.own_ref, f32[384,1024]{1,0:T(8,128)S(1)} %get-tuple-element.12.sum_ref, f32[384,128]{1,0:T(8,128)S(1)} %get-tuple-element.13.count_ref, bf16[3088,128]{1,0:T(8,128)(2,1)S(1)} %collective-permute-done.7.far_ref), custom_call_target="tpu_custom_call" | custom-call | flops 603979776 | bytes 1572864 | tf_op jit(solution)/shard_map/late/pallas_call | solution.py:216
Async XLA Ops:
  2.0 22.8 %collective-permute-start = (bf16[3088,128]{1,0:T(8,128)(2,1)S(1)}, bf16[3088,128]{1,0:T(8,128)(2,1)S(1)}, u32[]{:S(2)}, u32[]{:S(2)}) collective-permute-start(bf16[3088,128]{1,0:T(8,128)(2,1)S(1)} %pack.1.own_ref), channel_id=1, source_target_pairs={{0,2},{1,3},{2,0},{3,1},{4,6},{5,7},{6,4},{7,5},{8,10},{9,11},{10,... | collective-permute-start | bytes 2371592 | tf_op jit(solution)/shard_map/ppermute | solution.py:41
  7.1 27.9 %collective-permute-start.2 = (bf16[3088,128]{1,0:T(8,128)(2,1)S(1)}, bf16[3088,128]{1,0:T(8,128)(2,1)S(1)}, u32[]{:S(2)}, u32[]{:S(2)}) collective-permute-start(bf16[3088,128]{1,0:T(8,128)(2,1)S(1)} %pack.1.own_ref), channel_id=1, source_target_pairs={{0,4},{1,5},{2,6},{3,7},{4,8},{5,9},{6,10},{7,11},{8,12},{9,13},{1... | collective-permute-start | bytes 2371592 | tf_op jit(solution)/shard_map/ppermute | solution.py:41
  11.0 26.9 %collective-permute-start.1 = (bf16[3088,128]{1,0:T(8,128)(2,1)S(1)}, bf16[3088,128]{1,0:T(8,128)(2,1)S(1)}, u32[]{:S(2)}, u32[]{:S(2)}) collective-permute-start(bf16[3088,128]{1,0:T(8,128)(2,1)S(1)} %pack.1.own_ref), channel_id=1, source_target_pairs={{4,0},{5,1},{6,2},{7,3},{8,4},{9,5},{10,6},{11,7},{12,8},{13,9},{1... | collective-permute-start | bytes 2371592 | tf_op jit(solution)/shard_map/ppermute | solution.py:41
  19.9 23.0 %collective-permute-start.4 = (bf16[3088,128]{1,0:T(8,128)(2,1)S(1)}, bf16[3088,128]{1,0:T(8,128)(2,1)}, u32[]{:S(2)}, u32[]{:S(2)}) collective-permute-start(bf16[3088,128]{1,0:T(8,128)(2,1)S(1)} %pack.1.own_ref), channel_id=1, source_target_pairs={{0,1},{1,0},{2,3},{3,2},{4,5},{5,4},{6,7},{7,6},{8,9},{9,8},{10,11... | collective-permute-start | bytes 2371592 | tf_op jit(solution)/shard_map/ppermute | solution.py:41
  22.5 23.2 %collective-permute-start.3 = (bf16[3088,128]{1,0:T(8,128)(2,1)S(1)}, bf16[3088,128]{1,0:T(8,128)(2,1)}, u32[]{:S(2)}, u32[]{:S(2)}) collective-permute-start(bf16[3088,128]{1,0:T(8,128)(2,1)S(1)} %pack.1.own_ref), channel_id=1, source_target_pairs={{1,2},{2,1},{3,0},{0,3},{5,6},{6,5},{7,4},{4,7},{9,10},{10,9},{11,... | collective-permute-start | bytes 2371592 | tf_op jit(solution)/shard_map/ppermute | solution.py:41
  24.8 27.6 %collective-permute-start.5 = (bf16[3088,128]{1,0:T(8,128)(2,1)S(1)}, bf16[3088,128]{1,0:T(8,128)(2,1)S(1)}, u32[]{:S(2)}, u32[]{:S(2)}) collective-permute-start(bf16[3088,128]{1,0:T(8,128)(2,1)S(1)} %collective-permute-done.refs_0_), channel_id=1, source_target_pairs={{0,4},{1,5},{4,8},{5,9},{8,12},{9,13},{12,16},{13,17},{16,20},{17,... | collective-permute-start | bytes 2371592 | tf_op jit(solution)/shard_map/ppermute | solution.py:41
  38.0 21.5 %collective-permute-start.6 = (bf16[3088,128]{1,0:T(8,128)(2,1)S(1)}, bf16[3088,128]{1,0:T(8,128)(2,1)S(1)}, u32[]{:S(2)}, u32[]{:S(2)}) collective-permute-start(bf16[3088,128]{1,0:T(8,128)(2,1)S(1)} %get-tuple-element.15), channel_id=1, source_target_pairs={{0,1},{1,0},{2,3},{3,2},{4,5},{5,4},{6,7},{7,6},{8,9},{9,8},{10,11... | collective-permute-start | bytes 2371592 | tf_op jit(solution)/shard_map/ppermute | solution.py:41
  40.6 22.5 %collective-permute-start.7 = (bf16[3088,128]{1,0:T(8,128)(2,1)S(1)}, bf16[3088,128]{1,0:T(8,128)(2,1)S(1)}, u32[]{:S(2)}, u32[]{:S(2)}) collective-permute-start(bf16[3088,128]{1,0:T(8,128)(2,1)S(1)} %get-tuple-element.14), channel_id=1, source_target_pairs={{1,2},{2,1},{3,0},{0,3},{5,6},{6,5},{7,4},{4,7},{9,10},{10,9},{11,... | collective-permute-start | bytes 2371592 | tf_op jit(solution)/shard_map/ppermute | solution.py:41

commit v6 on v5

--- a/solution.py
+++ b/solution.py
@@ -15,7 +15,7 @@
 PARTS = 2
 LANES = 128
 TAIL = 16
-VMEM_BYTES = 40 * 1024 * 1024
+VMEM_BYTES = 20 * 1024 * 1024
 
 
 def plane_pairs(total, up, along, columns=range(RING)):

time: 65.5 us -> 65.5 us (level)
  no operation moved by 1% of the time
where the time goes in v6:
time: 65.5 us; the launch traced here: 65.2 us
  starting transfers between devices  32.6 us (50%)
  waiting for transfers between devices  19.3 us (29%)
  Pallas kernels  12.5 us (19%)
  between operations  0.77 us (1%)
    ppermute x8, starting transfers between devices, send(): return lax.ppermute(block, AXES, pairs)  32.6 us
    ppermute x8, waiting for transfers between devices, send(): return lax.ppermute(block, AXES, pairs)  19.3 us
    pallas_call x3, Pallas kernels, add(): pl.pallas_call(functools.partial(block_kernel, kernel_scale, not state),...  8.97 us
    pallas_call x1, Pallas kernels, shards(): pl.pallas_call(functools.partial(last_kernel, kernel_scale), out_shape=(s...  2.13 us
    pallas_call x1, Pallas kernels, shards(): pl.pallas_call(pack_kernel, out_shape=block, in_specs=[pl.BlockSpec(memor...  1.38 us
  transfers between devices with their start and end apart: 8, of which 5 were waited for; matrix products, arithmetic and copies ran while one was open for 0% of the time, Pallas kernels for 14%

profile of v6, /device:TPU:6, one launch (start us, length us, event | category | flops | bytes accessed | tf_op | source)
XLA Modules:
  0.0 65.2 jit_solution(2986855077008212827)
XLA Ops:
  0.6 1.4 %pack.1.own_ref = bf16[3088,128]{1,0:T(8,128)(2,1)S(1)} custom-call(bf16[384,1024]{1,0:T(8,128)(2,1)} %values_hbm.1, s32[384]{0:T(512)} %label_hbm.1), custom_call_target="tpu_custom_call" | custom-call | tf_op jit(solution)/shard_map/pack/pallas_call | solution.py:176
  2.0 5.1 %collective-permute-start = (bf16[3088,128]{1,0:T(8,128)(2,1)S(1)}, bf16[3088,128]{1,0:T(8,128)(2,1)S(1)}, u32[]{:S(2)}, u32[]{:S(2)}) collective-permute-start(bf16[3088,128]{1,0:T(8,128)(2,1)S(1)} %pack.1.own_ref), channel_id=1, source_target_pairs={{0,2},{1,3},{2,0},{3,1},{4,6},{5,7},{6,4},{7,5},{8,10},{9,11},{10,... | collective-permute-start | bytes 2371592 | tf_op jit(solution)/shard_map/ppermute | solution.py:41
  7.1 3.8 %collective-permute-start.2 = (bf16[3088,128]{1,0:T(8,128)(2,1)S(1)}, bf16[3088,128]{1,0:T(8,128)(2,1)S(1)}, u32[]{:S(2)}, u32[]{:S(2)}) collective-permute-start(bf16[3088,128]{1,0:T(8,128)(2,1)S(1)} %pack.1.own_ref), channel_id=1, source_target_pairs={{0,4},{1,5},{2,6},{3,7},{4,8},{5,9},{6,10},{7,11},{8,12},{9,13},{1... | collective-permute-start | bytes 2371592 | tf_op jit(solution)/shard_map/ppermute | solution.py:41
  11.0 8.9 %collective-permute-start.1 = (bf16[3088,128]{1,0:T(8,128)(2,1)S(1)}, bf16[3088,128]{1,0:T(8,128)(2,1)S(1)}, u32[]{:S(2)}, u32[]{:S(2)}) collective-permute-start(bf16[3088,128]{1,0:T(8,128)(2,1)S(1)} %pack.1.own_ref), channel_id=1, source_target_pairs={{4,0},{5,1},{6,2},{7,3},{8,4},{9,5},{10,6},{11,7},{12,8},{13,9},{1... | collective-permute-start | bytes 2371592 | tf_op jit(solution)/shard_map/ppermute | solution.py:41
  19.9 2.6 %collective-permute-start.4 = (bf16[3088,128]{1,0:T(8,128)(2,1)S(1)}, bf16[3088,128]{1,0:T(8,128)(2,1)}, u32[]{:S(2)}, u32[]{:S(2)}) collective-permute-start(bf16[3088,128]{1,0:T(8,128)(2,1)S(1)} %pack.1.own_ref), channel_id=1, source_target_pairs={{0,1},{1,0},{2,3},{3,2},{4,5},{5,4},{6,7},{7,6},{8,9},{9,8},{10,11... | collective-permute-start | bytes 2371592 | tf_op jit(solution)/shard_map/ppermute | solution.py:41
  22.5 2.3 %collective-permute-start.3 = (bf16[3088,128]{1,0:T(8,128)(2,1)S(1)}, bf16[3088,128]{1,0:T(8,128)(2,1)}, u32[]{:S(2)}, u32[]{:S(2)}) collective-permute-start(bf16[3088,128]{1,0:T(8,128)(2,1)S(1)} %pack.1.own_ref), channel_id=1, source_target_pairs={{1,2},{2,1},{3,0},{0,3},{5,6},{6,5},{7,4},{4,7},{9,10},{10,9},{11,... | collective-permute-start | bytes 2371592 | tf_op jit(solution)/shard_map/ppermute | solution.py:41
  24.8 0.0 collective-permute-done.refs_0_
  24.8 5.0 %collective-permute-start.5 = (bf16[3088,128]{1,0:T(8,128)(2,1)S(1)}, bf16[3088,128]{1,0:T(8,128)(2,1)S(1)}, u32[]{:S(2)}, u32[]{:S(2)}) collective-permute-start(bf16[3088,128]{1,0:T(8,128)(2,1)S(1)} %collective-permute-done.refs_0_), channel_id=1, source_target_pairs={{0,4},{1,5},{4,8},{5,9},{8,12},{9,13},{12,16},{13,17},{16,20},{17,... | collective-permute-start | bytes 2371592 | tf_op jit(solution)/shard_map/ppermute | solution.py:41
  29.8 5.2 %collective-permute-done.2.refs_2_ = bf16[3088,128]{1,0:T(8,128)(2,1)S(1)} collective-permute-done((bf16[3088,128]{1,0:T(8,128)(2,1)S(1)}, bf16[3088,128]{1,0:T(8,128)(2,1)S(1)}, u32[]{:S(2)}, u32[]{:S(2)}) %collective-permute-start.2) | collective-permute-done | bytes 790560 | tf_op jit(solution)/shard_map/ppermute | solution.py:41
  35.0 2.9 %collective-permute-done.1.refs_1_ = bf16[3088,128]{1,0:T(8,128)(2,1)S(1)} collective-permute-done((bf16[3088,128]{1,0:T(8,128)(2,1)S(1)}, bf16[3088,128]{1,0:T(8,128)(2,1)S(1)}, u32[]{:S(2)}, u32[]{:S(2)}) %collective-permute-start.1) | collective-permute-done | bytes 790560 | tf_op jit(solution)/shard_map/ppermute | solution.py:41
  37.9 0.1 broadcast_select_fusion
  38.0 2.6 %collective-permute-start.6 = (bf16[3088,128]{1,0:T(8,128)(2,1)S(1)}, bf16[3088,128]{1,0:T(8,128)(2,1)S(1)}, u32[]{:S(2)}, u32[]{:S(2)}) collective-permute-start(bf16[3088,128]{1,0:T(8,128)(2,1)S(1)} %get-tuple-element.15), channel_id=1, source_target_pairs={{0,1},{1,0},{2,3},{3,2},{4,5},{5,4},{6,7},{7,6},{8,9},{9,8},{10,11... | collective-permute-start | bytes 2371592 | tf_op jit(solution)/shard_map/ppermute | solution.py:41
  40.6 2.3 %collective-permute-start.7 = (bf16[3088,128]{1,0:T(8,128)(2,1)S(1)}, bf16[3088,128]{1,0:T(8,128)(2,1)S(1)}, u32[]{:S(2)}, u32[]{:S(2)}) collective-permute-start(bf16[3088,128]{1,0:T(8,128)(2,1)S(1)} %get-tuple-element.14), channel_id=1, source_target_pairs={{1,2},{2,1},{3,0},{0,3},{5,6},{6,5},{7,4},{4,7},{9,10},{10,9},{11,... | collective-permute-start | bytes 2371592 | tf_op jit(solution)/shard_map/ppermute | solution.py:41
  42.9 0.0 collective-permute-done.4.refs_4_
  42.9 2.7 %collective-permute-done.3.refs_3_ = bf16[3088,128]{1,0:T(8,128)(2,1)} collective-permute-done((bf16[3088,128]{1,0:T(8,128)(2,1)S(1)}, bf16[3088,128]{1,0:T(8,128)(2,1)}, u32[]{:S(2)}, u32[]{:S(2)}) %collective-permute-start.3) | collective-permute-done | bytes 790560 | tf_op jit(solution)/shard_map/ppermute | solution.py:41
  45.7 6.8 %near.1 = (f32[384,1024]{1,0:T(8,128)S(1)}, f32[384,128]{1,0:T(8,128)S(1)}) custom-call(bf16[3088,128]{1,0:T(8,128)(2,1)S(1)} %pack.1.own_ref, bf16[3088,128]{1,0:T(8,128)(2,1)S(1)} %collective-permute-done.refs_0_, bf16[3088,128]{1,0:T(8,128)(2,1)S(1)} %collective-permute-done.1.refs_1_, bf16[3088,128]{1,0:T(8,128)(2,1)S(1)} %collective-permute-done.2.refs_2_, ...), custom_call_target="tpu_custom_call" | custom-call | flops 3623878656 | bytes 5505024 | tf_op jit(solution)/shard_map/near/pallas_call | solution.py:194
  52.5 0.0 collective-permute-done.5.refs_2_
  52.5 1.1 %corner.1 = (f32[384,1024]{1,0:T(8,128)S(1)}, f32[384,128]{1,0:T(8,128)S(1)}) custom-call(bf16[3088,128]{1,0:T(8,128)(2,1)S(1)} %pack.1.own_ref, f32[384,1024]{1,0:T(8,128)S(1)} %get-tuple-element.8.refs_0_, f32[384,128]{1,0:T(8,128)S(1)} %get-tuple-element.9.refs_1_, bf16[3088,128]{1,0:T(8,128)(2,1)S(1)} %collective-permute-done.5.refs_2_), custom_call_target="tpu_custom_call" | custom-call | flops 603979776 | bytes 1572864 | tf_op jit(solution)/shard_map/corner/pallas_call | solution.py:194
  53.6 6.0 %collective-permute-done.6.refs_2_ = bf16[3088,128]{1,0:T(8,128)(2,1)S(1)} collective-permute-done((bf16[3088,128]{1,0:T(8,128)(2,1)S(1)}, bf16[3088,128]{1,0:T(8,128)(2,1)S(1)}, u32[]{:S(2)}, u32[]{:S(2)}) %collective-permute-start.6) | collective-permute-done | bytes 790560 | tf_op jit(solution)/shard_map/ppermute | solution.py:41
  59.5 1.1 %side.1 = (f32[384,1024]{1,0:T(8,128)S(1)}, f32[384,128]{1,0:T(8,128)S(1)}) custom-call(bf16[3088,128]{1,0:T(8,128)(2,1)S(1)} %pack.1.own_ref, f32[384,1024]{1,0:T(8,128)S(1)} %get-tuple-element.10.refs_0_, f32[384,128]{1,0:T(8,128)S(1)} %get-tuple-element.11.refs_1_, bf16[3088,128]{1,0:T(8,128)(2,1)S(1)} %collective-permute-done.6.refs_2_), custom_call_target="tpu_custom_call" | custom-call | flops 603979776 | bytes 1572864 | tf_op jit(solution)/shard_map/side/pallas_call | solution.py:194
  60.6 2.4 %collective-permute-done.7.far_ref = bf16[3088,128]{1,0:T(8,128)(2,1)S(1)} collective-permute-done((bf16[3088,128]{1,0:T(8,128)(2,1)S(1)}, bf16[3088,128]{1,0:T(8,128)(2,1)S(1)}, u32[]{:S(2)}, u32[]{:S(2)}) %collective-permute-start.7) | collective-permute-done | bytes 790560 | tf_op jit(solution)/shard_map/ppermute | solution.py:41
  63.1 2.1 %late.1 = (f32[384,1024]{1,0:T(8,128)}, f32[384]{0:T(512)}) custom-call(bf16[3088,128]{1,0:T(8,128)(2,1)S(1)} %pack.1.own_ref, f32[384,1024]{1,0:T(8,128)S(1)} %get-tuple-element.12.sum_ref, f32[384,128]{1,0:T(8,128)S(1)} %get-tuple-element.13.count_ref, bf16[3088,128]{1,0:T(8,128)(2,1)S(1)} %collective-permute-done.7.far_ref), custom_call_target="tpu_custom_call" | custom-call | flops 603979776 | bytes 1572864 | tf_op jit(solution)/shard_map/late/pallas_call | solution.py:216
Async XLA Ops:
  2.0 22.8 %collective-permute-start = (bf16[3088,128]{1,0:T(8,128)(2,1)S(1)}, bf16[3088,128]{1,0:T(8,128)(2,1)S(1)}, u32[]{:S(2)}, u32[]{:S(2)}) collective-permute-start(bf16[3088,128]{1,0:T(8,128)(2,1)S(1)} %pack.1.own_ref), channel_id=1, source_target_pairs={{0,2},{1,3},{2,0},{3,1},{4,6},{5,7},{6,4},{7,5},{8,10},{9,11},{10,... | collective-permute-start | bytes 2371592 | tf_op jit(solution)/shard_map/ppermute | solution.py:41
  7.1 27.9 %collective-permute-start.2 = (bf16[3088,128]{1,0:T(8,128)(2,1)S(1)}, bf16[3088,128]{1,0:T(8,128)(2,1)S(1)}, u32[]{:S(2)}, u32[]{:S(2)}) collective-permute-start(bf16[3088,128]{1,0:T(8,128)(2,1)S(1)} %pack.1.own_ref), channel_id=1, source_target_pairs={{0,4},{1,5},{2,6},{3,7},{4,8},{5,9},{6,10},{7,11},{8,12},{9,13},{1... | collective-permute-start | bytes 2371592 | tf_op jit(solution)/shard_map/ppermute | solution.py:41
  11.0 26.9 %collective-permute-start.1 = (bf16[3088,128]{1,0:T(8,128)(2,1)S(1)}, bf16[3088,128]{1,0:T(8,128)(2,1)S(1)}, u32[]{:S(2)}, u32[]{:S(2)}) collective-permute-start(bf16[3088,128]{1,0:T(8,128)(2,1)S(1)} %pack.1.own_ref), channel_id=1, source_target_pairs={{4,0},{5,1},{6,2},{7,3},{8,4},{9,5},{10,6},{11,7},{12,8},{13,9},{1... | collective-permute-start | bytes 2371592 | tf_op jit(solution)/shard_map/ppermute | solution.py:41
  19.9 23.0 %collective-permute-start.4 = (bf16[3088,128]{1,0:T(8,128)(2,1)S(1)}, bf16[3088,128]{1,0:T(8,128)(2,1)}, u32[]{:S(2)}, u32[]{:S(2)}) collective-permute-start(bf16[3088,128]{1,0:T(8,128)(2,1)S(1)} %pack.1.own_ref), channel_id=1, source_target_pairs={{0,1},{1,0},{2,3},{3,2},{4,5},{5,4},{6,7},{7,6},{8,9},{9,8},{10,11... | collective-permute-start | bytes 2371592 | tf_op jit(solution)/shard_map/ppermute | solution.py:41
  22.5 23.2 %collective-permute-start.3 = (bf16[3088,128]{1,0:T(8,128)(2,1)S(1)}, bf16[3088,128]{1,0:T(8,128)(2,1)}, u32[]{:S(2)}, u32[]{:S(2)}) collective-permute-start(bf16[3088,128]{1,0:T(8,128)(2,1)S(1)} %pack.1.own_ref), channel_id=1, source_target_pairs={{1,2},{2,1},{3,0},{0,3},{5,6},{6,5},{7,4},{4,7},{9,10},{10,9},{11,... | collective-permute-start | bytes 2371592 | tf_op jit(solution)/shard_map/ppermute | solution.py:41
  24.8 27.6 %collective-permute-start.5 = (bf16[3088,128]{1,0:T(8,128)(2,1)S(1)}, bf16[3088,128]{1,0:T(8,128)(2,1)S(1)}, u32[]{:S(2)}, u32[]{:S(2)}) collective-permute-start(bf16[3088,128]{1,0:T(8,128)(2,1)S(1)} %collective-permute-done.refs_0_), channel_id=1, source_target_pairs={{0,4},{1,5},{4,8},{5,9},{8,12},{9,13},{12,16},{13,17},{16,20},{17,... | collective-permute-start | bytes 2371592 | tf_op jit(solution)/shard_map/ppermute | solution.py:41
  38.0 21.5 %collective-permute-start.6 = (bf16[3088,128]{1,0:T(8,128)(2,1)S(1)}, bf16[3088,128]{1,0:T(8,128)(2,1)S(1)}, u32[]{:S(2)}, u32[]{:S(2)}) collective-permute-start(bf16[3088,128]{1,0:T(8,128)(2,1)S(1)} %get-tuple-element.15), channel_id=1, source_target_pairs={{0,1},{1,0},{2,3},{3,2},{4,5},{5,4},{6,7},{7,6},{8,9},{9,8},{10,11... | collective-permute-start | bytes 2371592 | tf_op jit(solution)/shard_map/ppermute | solution.py:41
  40.6 22.5 %collective-permute-start.7 = (bf16[3088,128]{1,0:T(8,128)(2,1)S(1)}, bf16[3088,128]{1,0:T(8,128)(2,1)S(1)}, u32[]{:S(2)}, u32[]{:S(2)}) collective-permute-start(bf16[3088,128]{1,0:T(8,128)(2,1)S(1)} %get-tuple-element.14), channel_id=1, source_target_pairs={{1,2},{2,1},{3,0},{0,3},{5,6},{6,5},{7,4},{4,7},{9,10},{10,9},{11,... | collective-permute-start | bytes 2371592 | tf_op jit(solution)/shard_map/ppermute | solution.py:41

commit v7 on v6

--- a/solution.py
+++ b/solution.py
@@ -210,7 +210,8 @@
     corner = send(across, climb)
     first_side = send(jnp.where(lax.rem(column, 2) == 1, below, above), ring_swaps(total, 0))
     second_side = send(jnp.where(column >= RING // 2, below, above), ring_swaps(total, 1))
-    state = add((), (across, above, below, second_column, first_column), "near")
+    state = add((), (across, below, above), "near")
+    state = add(state, (first_column, second_column), "columns")
     state = add(state, (corner,), "corner")
     state = add(state, (first_side,), "side")
     return pl.pallas_call(

time: 65.5 us -> 65.5 us (level)
    pallas_call x3 -> x4, Pallas kernels: 8.97 us -> 9.18 us  [add(): pl.pallas_call(functools.partial(block_kernel, kernel_scale, not state),...]
where the time goes in v7:
time: 65.5 us; the launch traced here: 65.2 us
  starting transfers between devices  32.6 us (50%)
  waiting for transfers between devices  19 us (29%)
  Pallas kernels  12.7 us (19%)
  between operations  0.77 us (1%)
    ppermute x8, starting transfers between devices, send(): return lax.ppermute(block, AXES, pairs)  32.6 us
    ppermute x8, waiting for transfers between devices, send(): return lax.ppermute(block, AXES, pairs)  19 us
    pallas_call x4, Pallas kernels, add(): pl.pallas_call(functools.partial(block_kernel, kernel_scale, not state),...  9.18 us
    pallas_call x1, Pallas kernels, shards(): pl.pallas_call(functools.partial(last_kernel, kernel_scale), out_shape=(s...  2.13 us
    pallas_call x1, Pallas kernels, shards(): pl.pallas_call(pack_kernel, out_shape=block, in_specs=[pl.BlockSpec(memor...  1.38 us
  transfers between devices with their start and end apart: 8, of which 5 were waited for; matrix products, arithmetic and copies ran while one was open for 0% of the time, Pallas kernels for 14%

profile of v7, /device:TPU:6, one launch (start us, length us, event | category | flops | bytes accessed | tf_op | source)
XLA Modules:
  0.0 65.2 jit_solution(16564860329894874947)
XLA Ops:
  0.6 1.4 %pack.1.own_ref = bf16[3088,128]{1,0:T(8,128)(2,1)S(1)} custom-call(bf16[384,1024]{1,0:T(8,128)(2,1)} %values_hbm.1, s32[384]{0:T(512)} %label_hbm.1), custom_call_target="tpu_custom_call" | custom-call | tf_op jit(solution)/shard_map/pack/pallas_call | solution.py:176
  2.0 5.1 %collective-permute-start = (bf16[3088,128]{1,0:T(8,128)(2,1)S(1)}, bf16[3088,128]{1,0:T(8,128)(2,1)S(1)}, u32[]{:S(2)}, u32[]{:S(2)}) collective-permute-start(bf16[3088,128]{1,0:T(8,128)(2,1)S(1)} %pack.1.own_ref), channel_id=1, source_target_pairs={{0,2},{1,3},{2,0},{3,1},{4,6},{5,7},{6,4},{7,5},{8,10},{9,11},{10,... | collective-permute-start | bytes 2371592 | tf_op jit(solution)/shard_map/ppermute | solution.py:41
  7.1 3.8 %collective-permute-start.1 = (bf16[3088,128]{1,0:T(8,128)(2,1)S(1)}, bf16[3088,128]{1,0:T(8,128)(2,1)S(1)}, u32[]{:S(2)}, u32[]{:S(2)}) collective-permute-start(bf16[3088,128]{1,0:T(8,128)(2,1)S(1)} %pack.1.own_ref), channel_id=1, source_target_pairs={{0,4},{1,5},{2,6},{3,7},{4,8},{5,9},{6,10},{7,11},{8,12},{9,13},{1... | collective-permute-start | bytes 2371592 | tf_op jit(solution)/shard_map/ppermute | solution.py:41
  11.0 8.9 %collective-permute-start.2 = (bf16[3088,128]{1,0:T(8,128)(2,1)S(1)}, bf16[3088,128]{1,0:T(8,128)(2,1)S(1)}, u32[]{:S(2)}, u32[]{:S(2)}) collective-permute-start(bf16[3088,128]{1,0:T(8,128)(2,1)S(1)} %pack.1.own_ref), channel_id=1, source_target_pairs={{4,0},{5,1},{6,2},{7,3},{8,4},{9,5},{10,6},{11,7},{12,8},{13,9},{1... | collective-permute-start | bytes 2371592 | tf_op jit(solution)/shard_map/ppermute | solution.py:41
  19.9 2.6 %collective-permute-start.3 = (bf16[3088,128]{1,0:T(8,128)(2,1)S(1)}, bf16[3088,128]{1,0:T(8,128)(2,1)}, u32[]{:S(2)}, u32[]{:S(2)}) collective-permute-start(bf16[3088,128]{1,0:T(8,128)(2,1)S(1)} %pack.1.own_ref), channel_id=1, source_target_pairs={{0,1},{1,0},{2,3},{3,2},{4,5},{5,4},{6,7},{7,6},{8,9},{9,8},{10,11... | collective-permute-start | bytes 2371592 | tf_op jit(solution)/shard_map/ppermute | solution.py:41
  22.5 2.3 %collective-permute-start.4 = (bf16[3088,128]{1,0:T(8,128)(2,1)S(1)}, bf16[3088,128]{1,0:T(8,128)(2,1)}, u32[]{:S(2)}, u32[]{:S(2)}) collective-permute-start(bf16[3088,128]{1,0:T(8,128)(2,1)S(1)} %pack.1.own_ref), channel_id=1, source_target_pairs={{1,2},{2,1},{3,0},{0,3},{5,6},{6,5},{7,4},{4,7},{9,10},{10,9},{11,... | collective-permute-start | bytes 2371592 | tf_op jit(solution)/shard_map/ppermute | solution.py:41
  24.8 0.0 collective-permute-done.refs_0_
  24.8 5.0 %collective-permute-start.5 = (bf16[3088,128]{1,0:T(8,128)(2,1)S(1)}, bf16[3088,128]{1,0:T(8,128)(2,1)S(1)}, u32[]{:S(2)}, u32[]{:S(2)}) collective-permute-start(bf16[3088,128]{1,0:T(8,128)(2,1)S(1)} %collective-permute-done.refs_0_), channel_id=1, source_target_pairs={{0,4},{1,5},{4,8},{5,9},{8,12},{9,13},{12,16},{13,17},{16,20},{17,... | collective-permute-start | bytes 2371592 | tf_op jit(solution)/shard_map/ppermute | solution.py:41
  29.8 5.2 %collective-permute-done.1.refs_1_ = bf16[3088,128]{1,0:T(8,128)(2,1)S(1)} collective-permute-done((bf16[3088,128]{1,0:T(8,128)(2,1)S(1)}, bf16[3088,128]{1,0:T(8,128)(2,1)S(1)}, u32[]{:S(2)}, u32[]{:S(2)}) %collective-permute-start.1) | collective-permute-done | bytes 790560 | tf_op jit(solution)/shard_map/ppermute | solution.py:41
  35.0 2.9 %collective-permute-done.2.refs_2_ = bf16[3088,128]{1,0:T(8,128)(2,1)S(1)} collective-permute-done((bf16[3088,128]{1,0:T(8,128)(2,1)S(1)}, bf16[3088,128]{1,0:T(8,128)(2,1)S(1)}, u32[]{:S(2)}, u32[]{:S(2)}) %collective-permute-start.2) | collective-permute-done | bytes 790560 | tf_op jit(solution)/shard_map/ppermute | solution.py:41
  37.9 0.1 broadcast_select_fusion
  38.0 2.6 %collective-permute-start.6 = (bf16[3088,128]{1,0:T(8,128)(2,1)S(1)}, bf16[3088,128]{1,0:T(8,128)(2,1)S(1)}, u32[]{:S(2)}, u32[]{:S(2)}) collective-permute-start(bf16[3088,128]{1,0:T(8,128)(2,1)S(1)} %get-tuple-element.19), channel_id=1, source_target_pairs={{0,1},{1,0},{2,3},{3,2},{4,5},{5,4},{6,7},{7,6},{8,9},{9,8},{10,11... | collective-permute-start | bytes 2371592 | tf_op jit(solution)/shard_map/ppermute | solution.py:41
  40.6 2.3 %collective-permute-start.7 = (bf16[3088,128]{1,0:T(8,128)(2,1)S(1)}, bf16[3088,128]{1,0:T(8,128)(2,1)S(1)}, u32[]{:S(2)}, u32[]{:S(2)}) collective-permute-start(bf16[3088,128]{1,0:T(8,128)(2,1)S(1)} %get-tuple-element.18), channel_id=1, source_target_pairs={{1,2},{2,1},{3,0},{0,3},{5,6},{6,5},{7,4},{4,7},{9,10},{10,9},{11,... | collective-permute-start | bytes 2371592 | tf_op jit(solution)/shard_map/ppermute | solution.py:41
  42.9 3.7 %near.1 = (f32[384,1024]{1,0:T(8,128)S(1)}, f32[384,128]{1,0:T(8,128)S(1)}) custom-call(bf16[3088,128]{1,0:T(8,128)(2,1)S(1)} %pack.1.own_ref, bf16[3088,128]{1,0:T(8,128)(2,1)S(1)} %collective-permute-done.refs_0_, bf16[3088,128]{1,0:T(8,128)(2,1)S(1)} %collective-permute-done.1.refs_1_, bf16[3088,128]{1,0:T(8,128)(2,1)S(1)} %collective-permute-done.2.refs_2_), custom_call_target="tpu_custom_call" | custom-call | flops 2415919104 | bytes 3932160 | tf_op jit(solution)/shard_map/near/pallas_call | solution.py:194
  46.6 0.0 collective-permute-done.3.refs_2_
  46.6 0.0 collective-permute-done.4.refs_3_
  46.6 3.3 %columns.1 = (f32[384,1024]{1,0:T(8,128)S(1)}, f32[384,128]{1,0:T(8,128)S(1)}) custom-call(bf16[3088,128]{1,0:T(8,128)(2,1)S(1)} %pack.1.own_ref, f32[384,1024]{1,0:T(8,128)S(1)} %get-tuple-element.10.refs_0_, f32[384,128]{1,0:T(8,128)S(1)} %get-tuple-element.11.refs_1_, bf16[3088,128]{1,0:T(8,128)(2,1)} %collective-permute-done.3.refs_2_, ...), custom_call_target="tpu_custom_call" | custom-call | flops 1207959552 | bytes 2359296 | tf_op jit(solution)/shard_map/columns/pallas_call | solution.py:194
  49.9 0.4 collective-permute-done.5.refs_2_
  50.3 1.1 %corner.1 = (f32[384,1024]{1,0:T(8,128)S(1)}, f32[384,128]{1,0:T(8,128)S(1)}) custom-call(bf16[3088,128]{1,0:T(8,128)(2,1)S(1)} %pack.1.own_ref, f32[384,1024]{1,0:T(8,128)S(1)} %get-tuple-element.12.refs_0_, f32[384,128]{1,0:T(8,128)S(1)} %get-tuple-element.13.refs_1_, bf16[3088,128]{1,0:T(8,128)(2,1)S(1)} %collective-permute-done.5.refs_2_), custom_call_target="tpu_custom_call" | custom-call | flops 603979776 | bytes 1572864 | tf_op jit(solution)/shard_map/corner/pallas_call | solution.py:194
  51.4 8.2 %collective-permute-done.6.refs_2_ = bf16[3088,128]{1,0:T(8,128)(2,1)S(1)} collective-permute-done((bf16[3088,128]{1,0:T(8,128)(2,1)S(1)}, bf16[3088,128]{1,0:T(8,128)(2,1)S(1)}, u32[]{:S(2)}, u32[]{:S(2)}) %collective-permute-start.6) | collective-permute-done | bytes 790560 | tf_op jit(solution)/shard_map/ppermute | solution.py:41
  59.5 1.1 %side.1 = (f32[384,1024]{1,0:T(8,128)S(1)}, f32[384,128]{1,0:T(8,128)S(1)}) custom-call(bf16[3088,128]{1,0:T(8,128)(2,1)S(1)} %pack.1.own_ref, f32[384,1024]{1,0:T(8,128)S(1)} %get-tuple-element.14.refs_0_, f32[384,128]{1,0:T(8,128)S(1)} %get-tuple-element.15.refs_1_, bf16[3088,128]{1,0:T(8,128)(2,1)S(1)} %collective-permute-done.6.refs_2_), custom_call_target="tpu_custom_call" | custom-call | flops 603979776 | bytes 1572864 | tf_op jit(solution)/shard_map/side/pallas_call | solution.py:194
  60.7 2.4 %collective-permute-done.7.far_ref = bf16[3088,128]{1,0:T(8,128)(2,1)S(1)} collective-permute-done((bf16[3088,128]{1,0:T(8,128)(2,1)S(1)}, bf16[3088,128]{1,0:T(8,128)(2,1)S(1)}, u32[]{:S(2)}, u32[]{:S(2)}) %collective-permute-start.7) | collective-permute-done | bytes 790560 | tf_op jit(solution)/shard_map/ppermute | solution.py:41
  63.1 2.1 %late.1 = (f32[384,1024]{1,0:T(8,128)}, f32[384]{0:T(512)}) custom-call(bf16[3088,128]{1,0:T(8,128)(2,1)S(1)} %pack.1.own_ref, f32[384,1024]{1,0:T(8,128)S(1)} %get-tuple-element.16.sum_ref, f32[384,128]{1,0:T(8,128)S(1)} %get-tuple-element.17.count_ref, bf16[3088,128]{1,0:T(8,128)(2,1)S(1)} %collective-permute-done.7.far_ref), custom_call_target="tpu_custom_call" | custom-call | flops 603979776 | bytes 1572864 | tf_op jit(solution)/shard_map/late/pallas_call | solution.py:217
Async XLA Ops:
  2.0 22.8 %collective-permute-start = (bf16[3088,128]{1,0:T(8,128)(2,1)S(1)}, bf16[3088,128]{1,0:T(8,128)(2,1)S(1)}, u32[]{:S(2)}, u32[]{:S(2)}) collective-permute-start(bf16[3088,128]{1,0:T(8,128)(2,1)S(1)} %pack.1.own_ref), channel_id=1, source_target_pairs={{0,2},{1,3},{2,0},{3,1},{4,6},{5,7},{6,4},{7,5},{8,10},{9,11},{10,... | collective-permute-start | bytes 2371592 | tf_op jit(solution)/shard_map/ppermute | solution.py:41
  7.1 27.9 %collective-permute-start.1 = (bf16[3088,128]{1,0:T(8,128)(2,1)S(1)}, bf16[3088,128]{1,0:T(8,128)(2,1)S(1)}, u32[]{:S(2)}, u32[]{:S(2)}) collective-permute-start(bf16[3088,128]{1,0:T(8,128)(2,1)S(1)} %pack.1.own_ref), channel_id=1, source_target_pairs={{0,4},{1,5},{2,6},{3,7},{4,8},{5,9},{6,10},{7,11},{8,12},{9,13},{1... | collective-permute-start | bytes 2371592 | tf_op jit(solution)/shard_map/ppermute | solution.py:41
  11.0 26.9 %collective-permute-start.2 = (bf16[3088,128]{1,0:T(8,128)(2,1)S(1)}, bf16[3088,128]{1,0:T(8,128)(2,1)S(1)}, u32[]{:S(2)}, u32[]{:S(2)}) collective-permute-start(bf16[3088,128]{1,0:T(8,128)(2,1)S(1)} %pack.1.own_ref), channel_id=1, source_target_pairs={{4,0},{5,1},{6,2},{7,3},{8,4},{9,5},{10,6},{11,7},{12,8},{13,9},{1... | collective-permute-start | bytes 2371592 | tf_op jit(solution)/shard_map/ppermute | solution.py:41
  19.9 26.7 %collective-permute-start.3 = (bf16[3088,128]{1,0:T(8,128)(2,1)S(1)}, bf16[3088,128]{1,0:T(8,128)(2,1)}, u32[]{:S(2)}, u32[]{:S(2)}) collective-permute-start(bf16[3088,128]{1,0:T(8,128)(2,1)S(1)} %pack.1.own_ref), channel_id=1, source_target_pairs={{0,1},{1,0},{2,3},{3,2},{4,5},{5,4},{6,7},{7,6},{8,9},{9,8},{10,11... | collective-permute-start | bytes 2371592 | tf_op jit(solution)/shard_map/ppermute | solution.py:41
  22.5 24.1 %collective-permute-start.4 = (bf16[3088,128]{1,0:T(8,128)(2,1)S(1)}, bf16[3088,128]{1,0:T(8,128)(2,1)}, u32[]{:S(2)}, u32[]{:S(2)}) collective-permute-start(bf16[3088,128]{1,0:T(8,128)(2,1)S(1)} %pack.1.own_ref), channel_id=1, source_target_pairs={{1,2},{2,1},{3,0},{0,3},{5,6},{6,5},{7,4},{4,7},{9,10},{10,9},{11,... | collective-permute-start | bytes 2371592 | tf_op jit(solution)/shard_map/ppermute | solution.py:41
  24.8 25.5 %collective-permute-start.5 = (bf16[3088,128]{1,0:T(8,128)(2,1)S(1)}, bf16[3088,128]{1,0:T(8,128)(2,1)S(1)}, u32[]{:S(2)}, u32[]{:S(2)}) collective-permute-start(bf16[3088,128]{1,0:T(8,128)(2,1)S(1)} %collective-permute-done.refs_0_), channel_id=1, source_target_pairs={{0,4},{1,5},{4,8},{5,9},{8,12},{9,13},{12,16},{13,17},{16,20},{17,... | collective-permute-start | bytes 2371592 | tf_op jit(solution)/shard_map/ppermute | solution.py:41
  38.0 21.5 %collective-permute-start.6 = (bf16[3088,128]{1,0:T(8,128)(2,1)S(1)}, bf16[3088,128]{1,0:T(8,128)(2,1)S(1)}, u32[]{:S(2)}, u32[]{:S(2)}) collective-permute-start(bf16[3088,128]{1,0:T(8,128)(2,1)S(1)} %get-tuple-element.19), channel_id=1, source_target_pairs={{0,1},{1,0},{2,3},{3,2},{4,5},{5,4},{6,7},{7,6},{8,9},{9,8},{10,11... | collective-permute-start | bytes 2371592 | tf_op jit(solution)/shard_map/ppermute | solution.py:41
  40.6 22.5 %collective-permute-start.7 = (bf16[3088,128]{1,0:T(8,128)(2,1)S(1)}, bf16[3088,128]{1,0:T(8,128)(2,1)S(1)}, u32[]{:S(2)}, u32[]{:S(2)}) collective-permute-start(bf16[3088,128]{1,0:T(8,128)(2,1)S(1)} %get-tuple-element.18), channel_id=1, source_target_pairs={{1,2},{2,1},{3,0},{0,3},{5,6},{6,5},{7,4},{4,7},{9,10},{10,9},{11,... | collective-permute-start | bytes 2371592 | tf_op jit(solution)/shard_map/ppermute | solution.py:41

commit v8 on v6

--- a/solution.py
+++ b/solution.py
@@ -49,15 +49,10 @@
         pltpu.make_async_copy(values_hbm.at[chunk], values_ref.at[chunk], semaphores.at[i])
         for i, chunk in enumerate(chunks)
     ]
-    label_copy.start()
     for copy in copies:
         copy.start()
+    label_copy.start()
     slabs = width // LANES
-    label_copy.wait()
-    label = (label_ref[...].reshape(1, rows) + 1).astype(jnp.float32)
-    lines = [label[:, i : i + LANES] for i in range(0, rows, LANES)]
-    blank = jnp.zeros((TAIL - len(lines), LANES), jnp.float32)
-    packed_ref[slabs * rows :, :] = jnp.concatenate([*lines, blank], axis=0).astype(jnp.bfloat16)
     for i, copy in enumerate(copies):
         copy.wait()
         values = values_ref[chunks[i], :].astype(jnp.float32)
@@ -66,6 +61,11 @@
         for slab in range(slabs):
             first = slab * rows + i * (rows // CHUNKS)
             packed_ref[first : first + rows // CHUNKS, :] = unit[:, slab * LANES : (slab + 1) * LANES]
+    label_copy.wait()
+    label = (label_ref[...].reshape(1, rows) + 1).astype(jnp.float32)
+    lines = [label[:, i : i + LANES] for i in range(0, rows, LANES)]
+    blank = jnp.zeros((TAIL - len(lines), LANES), jnp.float32)
+    packed_ref[slabs * rows :, :] = jnp.concatenate([*lines, blank], axis=0).astype(jnp.bfloat16)
 
 
 def rows_of(block_ref):

time: 65.5 us -> 65.5 us (level)
  no operation moved by 1% of the time
where the time goes in v8:
time: 65.5 us; the launch traced here: 65.2 us
  starting transfers between devices  32.6 us (50%)
  waiting for transfers between devices  19.2 us (29%)
  Pallas kernels  12.5 us (19%)
  between operations  0.77 us (1%)
    ppermute x8, starting transfers between devices, send(): return lax.ppermute(block, AXES, pairs)  32.6 us
    ppermute x8, waiting for transfers between devices, send(): return lax.ppermute(block, AXES, pairs)  19.2 us
    pallas_call x3, Pallas kernels, add(): pl.pallas_call(functools.partial(block_kernel, kernel_scale, not state),...  8.98 us
    pallas_call x1, Pallas kernels, shards(): pl.pallas_call(functools.partial(last_kernel, kernel_scale), out_shape=(s...  2.12 us
    pallas_call x1, Pallas kernels, shards(): pl.pallas_call(pack_kernel, out_shape=block, in_specs=[pl.BlockSpec(memor...  1.37 us
  transfers between devices with their start and end apart: 8, of which 5 were waited for; matrix products, arithmetic and copies ran while one was open for 0% of the time, Pallas kernels for 14%

profile of v8, /device:TPU:6, one launch (start us, length us, event | category | flops | bytes accessed | tf_op | source)
XLA Modules:
  0.0 65.2 jit_solution(14351304241867255643)
XLA Ops:
  0.6 1.4 %pack.1.own_ref = bf16[3088,128]{1,0:T(8,128)(2,1)S(1)} custom-call(bf16[384,1024]{1,0:T(8,128)(2,1)} %values_hbm.1, s32[384]{0:T(512)} %label_hbm.1), custom_call_target="tpu_custom_call" | custom-call | tf_op jit(solution)/shard_map/pack/pallas_call | solution.py:176
  2.0 5.1 %collective-permute-start = (bf16[3088,128]{1,0:T(8,128)(2,1)S(1)}, bf16[3088,128]{1,0:T(8,128)(2,1)S(1)}, u32[]{:S(2)}, u32[]{:S(2)}) collective-permute-start(bf16[3088,128]{1,0:T(8,128)(2,1)S(1)} %pack.1.own_ref), channel_id=1, source_target_pairs={{0,2},{1,3},{2,0},{3,1},{4,6},{5,7},{6,4},{7,5},{8,10},{9,11},{10,... | collective-permute-start | bytes 2371592 | tf_op jit(solution)/shard_map/ppermute | solution.py:41
  7.1 3.8 %collective-permute-start.2 = (bf16[3088,128]{1,0:T(8,128)(2,1)S(1)}, bf16[3088,128]{1,0:T(8,128)(2,1)S(1)}, u32[]{:S(2)}, u32[]{:S(2)}) collective-permute-start(bf16[3088,128]{1,0:T(8,128)(2,1)S(1)} %pack.1.own_ref), channel_id=1, source_target_pairs={{0,4},{1,5},{2,6},{3,7},{4,8},{5,9},{6,10},{7,11},{8,12},{9,13},{1... | collective-permute-start | bytes 2371592 | tf_op jit(solution)/shard_map/ppermute | solution.py:41
  11.0 8.9 %collective-permute-start.1 = (bf16[3088,128]{1,0:T(8,128)(2,1)S(1)}, bf16[3088,128]{1,0:T(8,128)(2,1)S(1)}, u32[]{:S(2)}, u32[]{:S(2)}) collective-permute-start(bf16[3088,128]{1,0:T(8,128)(2,1)S(1)} %pack.1.own_ref), channel_id=1, source_target_pairs={{4,0},{5,1},{6,2},{7,3},{8,4},{9,5},{10,6},{11,7},{12,8},{13,9},{1... | collective-permute-start | bytes 2371592 | tf_op jit(solution)/shard_map/ppermute | solution.py:41
  19.9 2.6 %collective-permute-start.4 = (bf16[3088,128]{1,0:T(8,128)(2,1)S(1)}, bf16[3088,128]{1,0:T(8,128)(2,1)}, u32[]{:S(2)}, u32[]{:S(2)}) collective-permute-start(bf16[3088,128]{1,0:T(8,128)(2,1)S(1)} %pack.1.own_ref), channel_id=1, source_target_pairs={{0,1},{1,0},{2,3},{3,2},{4,5},{5,4},{6,7},{7,6},{8,9},{9,8},{10,11... | collective-permute-start | bytes 2371592 | tf_op jit(solution)/shard_map/ppermute | solution.py:41
  22.5 2.3 %collective-permute-start.3 = (bf16[3088,128]{1,0:T(8,128)(2,1)S(1)}, bf16[3088,128]{1,0:T(8,128)(2,1)}, u32[]{:S(2)}, u32[]{:S(2)}) collective-permute-start(bf16[3088,128]{1,0:T(8,128)(2,1)S(1)} %pack.1.own_ref), channel_id=1, source_target_pairs={{1,2},{2,1},{3,0},{0,3},{5,6},{6,5},{7,4},{4,7},{9,10},{10,9},{11,... | collective-permute-start | bytes 2371592 | tf_op jit(solution)/shard_map/ppermute | solution.py:41
  24.8 0.0 collective-permute-done.refs_0_
  24.8 5.0 %collective-permute-start.5 = (bf16[3088,128]{1,0:T(8,128)(2,1)S(1)}, bf16[3088,128]{1,0:T(8,128)(2,1)S(1)}, u32[]{:S(2)}, u32[]{:S(2)}) collective-permute-start(bf16[3088,128]{1,0:T(8,128)(2,1)S(1)} %collective-permute-done.refs_0_), channel_id=1, source_target_pairs={{0,4},{1,5},{4,8},{5,9},{8,12},{9,13},{12,16},{13,17},{16,20},{17,... | collective-permute-start | bytes 2371592 | tf_op jit(solution)/shard_map/ppermute | solution.py:41
  29.8 5.2 %collective-permute-done.2.refs_2_ = bf16[3088,128]{1,0:T(8,128)(2,1)S(1)} collective-permute-done((bf16[3088,128]{1,0:T(8,128)(2,1)S(1)}, bf16[3088,128]{1,0:T(8,128)(2,1)S(1)}, u32[]{:S(2)}, u32[]{:S(2)}) %collective-permute-start.2) | collective-permute-done | bytes 790560 | tf_op jit(solution)/shard_map/ppermute | solution.py:41
  35.0 2.9 %collective-permute-done.1.refs_1_ = bf16[3088,128]{1,0:T(8,128)(2,1)S(1)} collective-permute-done((bf16[3088,128]{1,0:T(8,128)(2,1)S(1)}, bf16[3088,128]{1,0:T(8,128)(2,1)S(1)}, u32[]{:S(2)}, u32[]{:S(2)}) %collective-permute-start.1) | collective-permute-done | bytes 790560 | tf_op jit(solution)/shard_map/ppermute | solution.py:41
  37.9 0.1 broadcast_select_fusion
  38.0 2.6 %collective-permute-start.6 = (bf16[3088,128]{1,0:T(8,128)(2,1)S(1)}, bf16[3088,128]{1,0:T(8,128)(2,1)S(1)}, u32[]{:S(2)}, u32[]{:S(2)}) collective-permute-start(bf16[3088,128]{1,0:T(8,128)(2,1)S(1)} %get-tuple-element.15), channel_id=1, source_target_pairs={{0,1},{1,0},{2,3},{3,2},{4,5},{5,4},{6,7},{7,6},{8,9},{9,8},{10,11... | collective-permute-start | bytes 2371592 | tf_op jit(solution)/shard_map/ppermute | solution.py:41
  40.6 2.3 %collective-permute-start.7 = (bf16[3088,128]{1,0:T(8,128)(2,1)S(1)}, bf16[3088,128]{1,0:T(8,128)(2,1)S(1)}, u32[]{:S(2)}, u32[]{:S(2)}) collective-permute-start(bf16[3088,128]{1,0:T(8,128)(2,1)S(1)} %get-tuple-element.14), channel_id=1, source_target_pairs={{1,2},{2,1},{3,0},{0,3},{5,6},{6,5},{7,4},{4,7},{9,10},{10,9},{11,... | collective-permute-start | bytes 2371592 | tf_op jit(solution)/shard_map/ppermute | solution.py:41
  42.9 0.0 collective-permute-done.4.refs_4_
  42.9 2.7 %collective-permute-done.3.refs_3_ = bf16[3088,128]{1,0:T(8,128)(2,1)} collective-permute-done((bf16[3088,128]{1,0:T(8,128)(2,1)S(1)}, bf16[3088,128]{1,0:T(8,128)(2,1)}, u32[]{:S(2)}, u32[]{:S(2)}) %collective-permute-start.3) | collective-permute-done | bytes 790560 | tf_op jit(solution)/shard_map/ppermute | solution.py:41
  45.6 6.8 %near.1 = (f32[384,1024]{1,0:T(8,128)S(1)}, f32[384,128]{1,0:T(8,128)S(1)}) custom-call(bf16[3088,128]{1,0:T(8,128)(2,1)S(1)} %pack.1.own_ref, bf16[3088,128]{1,0:T(8,128)(2,1)S(1)} %collective-permute-done.refs_0_, bf16[3088,128]{1,0:T(8,128)(2,1)S(1)} %collective-permute-done.1.refs_1_, bf16[3088,128]{1,0:T(8,128)(2,1)S(1)} %collective-permute-done.2.refs_2_, ...), custom_call_target="tpu_custom_call" | custom-call | flops 3623878656 | bytes 5505024 | tf_op jit(solution)/shard_map/near/pallas_call | solution.py:194
  52.5 0.0 collective-permute-done.5.refs_2_
  52.5 1.1 %corner.1 = (f32[384,1024]{1,0:T(8,128)S(1)}, f32[384,128]{1,0:T(8,128)S(1)}) custom-call(bf16[3088,128]{1,0:T(8,128)(2,1)S(1)} %pack.1.own_ref, f32[384,1024]{1,0:T(8,128)S(1)} %get-tuple-element.8.refs_0_, f32[384,128]{1,0:T(8,128)S(1)} %get-tuple-element.9.refs_1_, bf16[3088,128]{1,0:T(8,128)(2,1)S(1)} %collective-permute-done.5.refs_2_), custom_call_target="tpu_custom_call" | custom-call | flops 603979776 | bytes 1572864 | tf_op jit(solution)/shard_map/corner/pallas_call | solution.py:194
  53.6 6.0 %collective-permute-done.6.refs_2_ = bf16[3088,128]{1,0:T(8,128)(2,1)S(1)} collective-permute-done((bf16[3088,128]{1,0:T(8,128)(2,1)S(1)}, bf16[3088,128]{1,0:T(8,128)(2,1)S(1)}, u32[]{:S(2)}, u32[]{:S(2)}) %collective-permute-start.6) | collective-permute-done | bytes 790560 | tf_op jit(solution)/shard_map/ppermute | solution.py:41
  59.5 1.1 %side.1 = (f32[384,1024]{1,0:T(8,128)S(1)}, f32[384,128]{1,0:T(8,128)S(1)}) custom-call(bf16[3088,128]{1,0:T(8,128)(2,1)S(1)} %pack.1.own_ref, f32[384,1024]{1,0:T(8,128)S(1)} %get-tuple-element.10.refs_0_, f32[384,128]{1,0:T(8,128)S(1)} %get-tuple-element.11.refs_1_, bf16[3088,128]{1,0:T(8,128)(2,1)S(1)} %collective-permute-done.6.refs_2_), custom_call_target="tpu_custom_call" | custom-call | flops 603979776 | bytes 1572864 | tf_op jit(solution)/shard_map/side/pallas_call | solution.py:194
  60.6 2.4 %collective-permute-done.7.far_ref = bf16[3088,128]{1,0:T(8,128)(2,1)S(1)} collective-permute-done((bf16[3088,128]{1,0:T(8,128)(2,1)S(1)}, bf16[3088,128]{1,0:T(8,128)(2,1)S(1)}, u32[]{:S(2)}, u32[]{:S(2)}) %collective-permute-start.7) | collective-permute-done | bytes 790560 | tf_op jit(solution)/shard_map/ppermute | solution.py:41
  63.1 2.1 %late.1 = (f32[384,1024]{1,0:T(8,128)}, f32[384]{0:T(512)}) custom-call(bf16[3088,128]{1,0:T(8,128)(2,1)S(1)} %pack.1.own_ref, f32[384,1024]{1,0:T(8,128)S(1)} %get-tuple-element.12.sum_ref, f32[384,128]{1,0:T(8,128)S(1)} %get-tuple-element.13.count_ref, bf16[3088,128]{1,0:T(8,128)(2,1)S(1)} %collective-permute-done.7.far_ref), custom_call_target="tpu_custom_call" | custom-call | flops 603979776 | bytes 1572864 | tf_op jit(solution)/shard_map/late/pallas_call | solution.py:216
Async XLA Ops:
  2.0 22.8 %collective-permute-start = (bf16[3088,128]{1,0:T(8,128)(2,1)S(1)}, bf16[3088,128]{1,0:T(8,128)(2,1)S(1)}, u32[]{:S(2)}, u32[]{:S(2)}) collective-permute-start(bf16[3088,128]{1,0:T(8,128)(2,1)S(1)} %pack.1.own_ref), channel_id=1, source_target_pairs={{0,2},{1,3},{2,0},{3,1},{4,6},{5,7},{6,4},{7,5},{8,10},{9,11},{10,... | collective-permute-start | bytes 2371592 | tf_op jit(solution)/shard_map/ppermute | solution.py:41
  7.1 27.9 %collective-permute-start.2 = (bf16[3088,128]{1,0:T(8,128)(2,1)S(1)}, bf16[3088,128]{1,0:T(8,128)(2,1)S(1)}, u32[]{:S(2)}, u32[]{:S(2)}) collective-permute-start(bf16[3088,128]{1,0:T(8,128)(2,1)S(1)} %pack.1.own_ref), channel_id=1, source_target_pairs={{0,4},{1,5},{2,6},{3,7},{4,8},{5,9},{6,10},{7,11},{8,12},{9,13},{1... | collective-permute-start | bytes 2371592 | tf_op jit(solution)/shard_map/ppermute | solution.py:41
  11.0 26.9 %collective-permute-start.1 = (bf16[3088,128]{1,0:T(8,128)(2,1)S(1)}, bf16[3088,128]{1,0:T(8,128)(2,1)S(1)}, u32[]{:S(2)}, u32[]{:S(2)}) collective-permute-start(bf16[3088,128]{1,0:T(8,128)(2,1)S(1)} %pack.1.own_ref), channel_id=1, source_target_pairs={{4,0},{5,1},{6,2},{7,3},{8,4},{9,5},{10,6},{11,7},{12,8},{13,9},{1... | collective-permute-start | bytes 2371592 | tf_op jit(solution)/shard_map/ppermute | solution.py:41
  19.9 23.0 %collective-permute-start.4 = (bf16[3088,128]{1,0:T(8,128)(2,1)S(1)}, bf16[3088,128]{1,0:T(8,128)(2,1)}, u32[]{:S(2)}, u32[]{:S(2)}) collective-permute-start(bf16[3088,128]{1,0:T(8,128)(2,1)S(1)} %pack.1.own_ref), channel_id=1, source_target_pairs={{0,1},{1,0},{2,3},{3,2},{4,5},{5,4},{6,7},{7,6},{8,9},{9,8},{10,11... | collective-permute-start | bytes 2371592 | tf_op jit(solution)/shard_map/ppermute | solution.py:41
  22.5 23.2 %collective-permute-start.3 = (bf16[3088,128]{1,0:T(8,128)(2,1)S(1)}, bf16[3088,128]{1,0:T(8,128)(2,1)}, u32[]{:S(2)}, u32[]{:S(2)}) collective-permute-start(bf16[3088,128]{1,0:T(8,128)(2,1)S(1)} %pack.1.own_ref), channel_id=1, source_target_pairs={{1,2},{2,1},{3,0},{0,3},{5,6},{6,5},{7,4},{4,7},{9,10},{10,9},{11,... | collective-permute-start | bytes 2371592 | tf_op jit(solution)/shard_map/ppermute | solution.py:41
  24.8 27.7 %collective-permute-start.5 = (bf16[3088,128]{1,0:T(8,128)(2,1)S(1)}, bf16[3088,128]{1,0:T(8,128)(2,1)S(1)}, u32[]{:S(2)}, u32[]{:S(2)}) collective-permute-start(bf16[3088,128]{1,0:T(8,128)(2,1)S(1)} %collective-permute-done.refs_0_), channel_id=1, source_target_pairs={{0,4},{1,5},{4,8},{5,9},{8,12},{9,13},{12,16},{13,17},{16,20},{17,... | collective-permute-start | bytes 2371592 | tf_op jit(solution)/shard_map/ppermute | solution.py:41
  38.0 21.5 %collective-permute-start.6 = (bf16[3088,128]{1,0:T(8,128)(2,1)S(1)}, bf16[3088,128]{1,0:T(8,128)(2,1)S(1)}, u32[]{:S(2)}, u32[]{:S(2)}) collective-permute-start(bf16[3088,128]{1,0:T(8,128)(2,1)S(1)} %get-tuple-element.15), channel_id=1, source_target_pairs={{0,1},{1,0},{2,3},{3,2},{4,5},{5,4},{6,7},{7,6},{8,9},{9,8},{10,11... | collective-permute-start | bytes 2371592 | tf_op jit(solution)/shard_map/ppermute | solution.py:41
  40.6 22.5 %collective-permute-start.7 = (bf16[3088,128]{1,0:T(8,128)(2,1)S(1)}, bf16[3088,128]{1,0:T(8,128)(2,1)S(1)}, u32[]{:S(2)}, u32[]{:S(2)}) collective-permute-start(bf16[3088,128]{1,0:T(8,128)(2,1)S(1)} %get-tuple-element.14), channel_id=1, source_target_pairs={{1,2},{2,1},{3,0},{0,3},{5,6},{6,5},{7,4},{4,7},{9,10},{10,9},{11,... | collective-permute-start | bytes 2371592 | tf_op jit(solution)/shard_map/ppermute | solution.py:41
